TPU v7x, 32 devices: a whole 2x2x4 slice. The times are simulated.
32 devices in a mesh: ctx: 16 (over z, y, core), mp: 2 (over x).
Axes of the slice: x: 2, y: 2, z: 4, core: 2. Of those that a mesh axis runs over, the one named last changes fastest.
Arguments:
- proj: bfloat16 [4096, 3, 8192], P(('ctx', 'mp')), may hold values from -6 to 6
- conv_weight: float32 [3, 7, 8192], replicated, may hold values from -2 to 2
- residues: float32 [128, 16], P('mp'), may hold values from -1.5 to 1.5
- decays: float32 [128, 16], P('mp'), may hold values from 2.4414063e-05 to 0.03
- doc_lengths: int32 [32], replicated, may hold values from 1 to 768, 4096 in all
Outputs:
- mixed: bfloat16 [4096, 8192], P(('ctx', 'mp'))
All inputs are finite; a program needn't handle non-finite values.
Results may differ from a plain program's by a relative error of at most 0.014.
Values may be sent and summed in bfloat16 or wider, within the bound.
A program may use at most 128 MiB of HBM per device.

v0:
```python
import jax
import jax.numpy as jnp
from jax import lax
from jax.sharding import PartitionSpec as P


def shifted_2(block, axis, distance):
    devices = range(lax.axis_size(axis))
    route = [(i - distance, i) for i in devices if i - distance in devices]
    return lax.ppermute(block, axis, route)


def document_number_index(doc_lengths, positions):
    doc_starts = jnp.cumsum(doc_lengths) - doc_lengths
    inside = (doc_starts[None, :] <= positions[:, None]).astype(jnp.int32)
    return jnp.sum(inside, axis=1) - 1


def short_convolution(padded, conv_weight, padded_document_ids, padded_pos, out_rows):
    kernel_len = conv_weight.shape[1]
    result = jnp.zeros((out_rows,) + padded.shape[1:], jnp.float32)
    own_docs = padded_document_ids[kernel_len - 1 :]
    for position_shift in range(kernel_len):
        begin_row = kernel_len - 1 - position_shift
        earlier = padded[begin_row : begin_row + out_rows].astype(jnp.float32)
        keep_mask = (padded_document_ids[begin_row : begin_row + out_rows] == own_docs) & (
            padded_pos[begin_row : begin_row + out_rows] >= 0
        )
        result = (
            result
            + conv_weight[:, position_shift, :][None]
            * earlier
            * keep_mask.astype(jnp.float32)[:, None, None]
        )
    return result


def filter_tile(coefficient, decays, out_index, piece_start, width_in):
    span = float(width_in)
    out_float = (out_index - piece_start).astype(jnp.float32)
    shifted = jnp.maximum(out_float - span, -span)
    left_neighbor = coefficient[:, :, None] * jnp.exp(-decays[:, :, None] * shifted[None, None, :])
    in_offsets = jnp.arange(width_in).astype(jnp.float32)
    right_neighbor = jnp.exp(-decays[:, :, None] * (span - in_offsets)[None, None, :])
    token_tile_rows = jnp.einsum(
        "ejz,ejx->ezx", left_neighbor, right_neighbor, precision=lax.Precision.HIGHEST
    )
    lag_matrix = (out_index - piece_start)[:, None] - jnp.arange(width_in, dtype=jnp.int32)[None, :]
    return jnp.where((lag_matrix >= 0)[None], token_tile_rows, 0.0)


def split_product(form, weights, inputs):
    upper_part = weights.astype(jnp.bfloat16)
    lower_part = (weights - upper_part.astype(jnp.float32)).astype(jnp.bfloat16)
    first = jnp.einsum(form, upper_part, inputs, preferred_element_type=jnp.float32)
    return first + jnp.einsum(form, lower_part, inputs, preferred_element_type=jnp.float32)


def long_filter(product, residues, decays, block_begin_position):
    block_len = product.shape[0]
    channels = product.shape[1]
    group_count = residues.shape[0]
    group_width = channels // group_count
    coefficient = residues * jnp.sqrt(decays)
    out_index = block_begin_position + jnp.arange(block_len, dtype=jnp.int32)

    def one_tile(running, rows_part, part_start):
        width_in = rows_part.shape[0]
        token_tile_rows = filter_tile(coefficient, decays, out_index, part_start, width_in)
        inputs = rows_part.reshape(width_in, group_count, group_width)
        return running + split_product("grs,sgc->rgc", token_tile_rows, inputs)

    initial = jnp.zeros((block_len, group_count, group_width), jnp.float32)
    piece_rows = lax.all_gather(product, "ctx", axis=0, tiled=True)
    width_in = piece_rows.shape[0]
    count_blocks = width_in // block_len
    stacked = piece_rows.reshape(count_blocks, block_len, channels)
    starts = block_len * jnp.arange(count_blocks, dtype=jnp.int32)

    def scan_step(carry, pair):
        return (one_tile(carry, pair[0], pair[1]), None)

    result, unused = lax.scan(scan_step, initial, (stacked, starts))
    return result.reshape(block_len, channels).astype(jnp.bfloat16)


def shards(proj, conv_weight, residues, decays, doc_lengths):
    kernel_len = conv_weight.shape[1]
    channel_rows = lax.all_to_all(proj, "mp", split_axis=2, concat_axis=0, tiled=True)
    block_len = channel_rows.shape[0]
    channels = channel_rows.shape[2]
    local_weight = lax.dynamic_slice_in_dim(
        conv_weight, lax.axis_index("mp") * channels, channels, 2
    )
    tail_rows = shifted_2(channel_rows[block_len - (kernel_len - 1) :], "ctx", 1)
    block_begin_position = lax.axis_index("ctx") * block_len
    padded_pos = (
        block_begin_position
        - (kernel_len - 1)
        + jnp.arange(block_len + kernel_len - 1, dtype=jnp.int32)
    )
    padded_document_ids = document_number_index(doc_lengths, padded_pos)
    padded = jnp.concatenate([tail_rows, channel_rows], axis=0)
    conv = short_convolution(padded, local_weight, padded_document_ids, padded_pos, block_len)
    query_part = conv[:, 0]
    product = (conv[:, 1] * conv[:, 2]).astype(jnp.bfloat16)
    filtered = long_filter(product, residues, decays, block_begin_position)
    mixed_out = (query_part * filtered.astype(jnp.float32)).astype(jnp.bfloat16)
    return lax.all_to_all(mixed_out, "mp", split_axis=0, concat_axis=1, tiled=True)


def solution(mesh):
    return jax.shard_map(
        shards,
        mesh=mesh,
        in_specs=(P(("ctx", "mp"), None, None), P(), P("mp", None), P("mp", None), P()),
        out_specs=P(("ctx", "mp"), None),
        check_vma=False,
    )
```

profile of v0, /device:TPU:1, one launch (start us, length us, event | category | flops | bytes accessed | tf_op | source)
XLA Modules:
  0.0 1181.2 jit_solution(15968936817354822597)
XLA Ops:
  6.5 13.1 %copy.38 = bf16[128,3,8192]{0,1,2:T(4,128)(2,1)} copy(bf16[128,3,8192]{2,0,1:T(8,128)(2,1)} %param.7) | data formatting | bytes 12582912 | tf_op args[0]
  19.7 6.9 all-to-all-start
  30.8 88.5 %all-to-all-done = bf16[128,3,8192]{0,1,2:T(4,128)(2,1)} async-done(((bf16[128,3,8192]{0,1,2:T(4,128)(2,1)}), bf16[128,3,8192]{0,1,2:T(4,128)(2,1)}, u32[]{:S(2)}, u32[]{:S(2)}) %all-to-all-start) | async-done | bytes 6291488 | tf_op jit(solution)/shard_map/all_to_all | solution.py:89
  119.3 7.0 copy.39
  126.3 8.8 copy.40
  136.0 4.5 collective-permute-start
  143.1 27.9 %multiply_add_fusion = f32[256,3,4096]{2,0,1:T(8,128)S(1)} fusion(bf16[256,3,4096]{2,0,1:T(8,128)(2,1)} %bitcast.50, bf16[6,3,4096]{2,0,1:T(8,128)(2,1)S(1)} %collective-permute-done, f32[256]{0:T(256)S(1)} %get-tuple-element.180, f32[3,4096]{1,0:T(4,128)S(1)} %get-tuple-element.185, f32[256]{0:T(256)S(1)} %get-tuple-element.181, ...), kind=kLoop, calls=%fused_computation.32 | loop fusion | flops 141557760 | bytes 19373056 | tf_op jit(solution)/shard_map/add | solution.py:30
  171.1 3.5 fusion.25
  174.9 169.4 %all-gather.3.cloned.1.call-done = bf16[4096,1,4096]{2,0,1:T(8,128)(2,1)} async-done(((bf16[256,1,4096]{2,0,1:T(8,128)(2,1)}), bf16[4096,1,4096]{2,0,1:T(8,128)(2,1)}) %all-gather.3.cloned.1.call-update) | async-done | bytes 33554448 | tf_op jit(solution)/shard_map/all_gather | solution.py:74
  344.3 774.6 %while.13 = (s32[]{:T(128)}, f32[256,64,64]{0,2,1:T(8,128)}, bf16[16,256,4096]{2,1,0:T(8,128)(2,1)}, s32[16]{0:T(128)S(1)}, f32[64,16]{1,0:T(8,128)S(1)}, /*inde...) while((s32[]{:T(128)}, f32[256,64,64]{0,2,1:T(8,128)}, ...), condition=%wide.region_3.4_spmd.clone, body=%wide.region_2.3_spmd.clone.sunk | while | flops 1908279552 | bytes 79902864 | solution.py:83
  352.7 16.9 %fusion.38 = f32[64,256,256]{2,1,0:T(8,128)} fusion(f32[256]{0:T(256)S(1)} %get-tuple-element.236, f32[256]{0:T(256)S(1)} %get-tuple-element.237, f32[64,16]{1,0:T(8,128)S(1)} %bitcast.53, f32[64,16]{1,0:T(8,128)S(1)} %get-tuple-element.260), kind=kOutput, calls=%fused_computation.10.clone.1 | convolution fusion | flops 806092800 | bytes 16787456 | tf_op jit(solution)/shard_map/while/body/eval_jaxpr/ejz,ejx->ezx/dot_general | solution.py:45
  369.6 10.4 fusion.39
  380.0 11.6 bitcast_add_fusion.2
  400.0 16.9 %fusion.38 = f32[64,256,256]{2,1,0:T(8,128)} fusion(f32[256]{0:T(256)S(1)} %get-tuple-element.236, f32[256]{0:T(256)S(1)} %get-tuple-element.237, f32[64,16]{1,0:T(8,128)S(1)} %bitcast.53, f32[64,16]{1,0:T(8,128)S(1)} %get-tuple-element.260), kind=kOutput, calls=%fused_computation.10.clone.1 | convolution fusion | flops 806092800 | bytes 16787456 | tf_op jit(solution)/shard_map/while/body/eval_jaxpr/ejz,ejx->ezx/dot_general | solution.py:45
  416.9 10.4 fusion.39
  427.3 12.8 %bitcast_add_fusion.2 = f32[256,64,64]{0,2,1:T(8,128)} fusion(f32[256,64,64]{0,2,1:T(8,128)} %get-tuple-element.248, f32[64,64,256]{2,1,0:T(8,128)} %fusion.39, pred[]{:T(512)S(6)} %compare.3, bf16[256,64,64]{0,2,1:T(8,128)(2,1)S(1)} %bitcast.48, f32[64,256,256]{2,1,0:T(8,128)} %fusion.38, pred[256,256]{1,0:T(8,128)(4,1)S(1)} %subtract_compare_fusion.2), kind=kOutput, calls=%fused_computation.9.clone.1 | convolution fusion | flops 560988160 | bytes 31522816 | tf_op jit(solution)/shard_map/while/body/eval_jaxpr/grs,sgc->rgc/dot_general | solution.py:56
  448.5 16.9 %fusion.38 = f32[64,256,256]{2,1,0:T(8,128)} fusion(f32[256]{0:T(256)S(1)} %get-tuple-element.236, f32[256]{0:T(256)S(1)} %get-tuple-element.237, f32[64,16]{1,0:T(8,128)S(1)} %bitcast.53, f32[64,16]{1,0:T(8,128)S(1)} %get-tuple-element.260), kind=kOutput, calls=%fused_computation.10.clone.1 | convolution fusion | flops 806092800 | bytes 16787456 | tf_op jit(solution)/shard_map/while/body/eval_jaxpr/ejz,ejx->ezx/dot_general | solution.py:45
  465.3 10.4 fusion.39
  475.7 12.8 %bitcast_add_fusion.2 = f32[256,64,64]{0,2,1:T(8,128)} fusion(f32[256,64,64]{0,2,1:T(8,128)} %get-tuple-element.248, f32[64,64,256]{2,1,0:T(8,128)} %fusion.39, pred[]{:T(512)S(6)} %compare.3, bf16[256,64,64]{0,2,1:T(8,128)(2,1)S(1)} %bitcast.48, f32[64,256,256]{2,1,0:T(8,128)} %fusion.38, pred[256,256]{1,0:T(8,128)(4,1)S(1)} %subtract_compare_fusion.2), kind=kOutput, calls=%fused_computation.9.clone.1 | convolution fusion | flops 560988160 | bytes 31522816 | tf_op jit(solution)/shard_map/while/body/eval_jaxpr/grs,sgc->rgc/dot_general | solution.py:56
  497.0 16.9 %fusion.38 = f32[64,256,256]{2,1,0:T(8,128)} fusion(f32[256]{0:T(256)S(1)} %get-tuple-element.236, f32[256]{0:T(256)S(1)} %get-tuple-element.237, f32[64,16]{1,0:T(8,128)S(1)} %bitcast.53, f32[64,16]{1,0:T(8,128)S(1)} %get-tuple-element.260), kind=kOutput, calls=%fused_computation.10.clone.1 | convolution fusion | flops 806092800 | bytes 16787456 | tf_op jit(solution)/shard_map/while/body/eval_jaxpr/ejz,ejx->ezx/dot_general | solution.py:45
  513.8 10.4 fusion.39
  524.2 12.8 %bitcast_add_fusion.2 = f32[256,64,64]{0,2,1:T(8,128)} fusion(f32[256,64,64]{0,2,1:T(8,128)} %get-tuple-element.248, f32[64,64,256]{2,1,0:T(8,128)} %fusion.39, pred[]{:T(512)S(6)} %compare.3, bf16[256,64,64]{0,2,1:T(8,128)(2,1)S(1)} %bitcast.48, f32[64,256,256]{2,1,0:T(8,128)} %fusion.38, pred[256,256]{1,0:T(8,128)(4,1)S(1)} %subtract_compare_fusion.2), kind=kOutput, calls=%fused_computation.9.clone.1 | convolution fusion | flops 560988160 | bytes 31522816 | tf_op jit(solution)/shard_map/while/body/eval_jaxpr/grs,sgc->rgc/dot_general | solution.py:56
  545.5 16.9 %fusion.38 = f32[64,256,256]{2,1,0:T(8,128)} fusion(f32[256]{0:T(256)S(1)} %get-tuple-element.236, f32[256]{0:T(256)S(1)} %get-tuple-element.237, f32[64,16]{1,0:T(8,128)S(1)} %bitcast.53, f32[64,16]{1,0:T(8,128)S(1)} %get-tuple-element.260), kind=kOutput, calls=%fused_computation.10.clone.1 | convolution fusion | flops 806092800 | bytes 16787456 | tf_op jit(solution)/shard_map/while/body/eval_jaxpr/ejz,ejx->ezx/dot_general | solution.py:45
  562.3 10.4 fusion.39
  572.7 12.8 %bitcast_add_fusion.2 = f32[256,64,64]{0,2,1:T(8,128)} fusion(f32[256,64,64]{0,2,1:T(8,128)} %get-tuple-element.248, f32[64,64,256]{2,1,0:T(8,128)} %fusion.39, pred[]{:T(512)S(6)} %compare.3, bf16[256,64,64]{0,2,1:T(8,128)(2,1)S(1)} %bitcast.48, f32[64,256,256]{2,1,0:T(8,128)} %fusion.38, pred[256,256]{1,0:T(8,128)(4,1)S(1)} %subtract_compare_fusion.2), kind=kOutput, calls=%fused_computation.9.clone.1 | convolution fusion | flops 560988160 | bytes 31522816 | tf_op jit(solution)/shard_map/while/body/eval_jaxpr/grs,sgc->rgc/dot_general | solution.py:56
  593.9 16.9 %fusion.38 = f32[64,256,256]{2,1,0:T(8,128)} fusion(f32[256]{0:T(256)S(1)} %get-tuple-element.236, f32[256]{0:T(256)S(1)} %get-tuple-element.237, f32[64,16]{1,0:T(8,128)S(1)} %bitcast.53, f32[64,16]{1,0:T(8,128)S(1)} %get-tuple-element.260), kind=kOutput, calls=%fused_computation.10.clone.1 | convolution fusion | flops 806092800 | bytes 16787456 | tf_op jit(solution)/shard_map/while/body/eval_jaxpr/ejz,ejx->ezx/dot_general | solution.py:45
  610.8 10.4 fusion.39
  621.2 12.8 %bitcast_add_fusion.2 = f32[256,64,64]{0,2,1:T(8,128)} fusion(f32[256,64,64]{0,2,1:T(8,128)} %get-tuple-element.248, f32[64,64,256]{2,1,0:T(8,128)} %fusion.39, pred[]{:T(512)S(6)} %compare.3, bf16[256,64,64]{0,2,1:T(8,128)(2,1)S(1)} %bitcast.48, f32[64,256,256]{2,1,0:T(8,128)} %fusion.38, pred[256,256]{1,0:T(8,128)(4,1)S(1)} %subtract_compare_fusion.2), kind=kOutput, calls=%fused_computation.9.clone.1 | convolution fusion | flops 560988160 | bytes 31522816 | tf_op jit(solution)/shard_map/while/body/eval_jaxpr/grs,sgc->rgc/dot_general | solution.py:56
  642.4 16.9 %fusion.38 = f32[64,256,256]{2,1,0:T(8,128)} fusion(f32[256]{0:T(256)S(1)} %get-tuple-element.236, f32[256]{0:T(256)S(1)} %get-tuple-element.237, f32[64,16]{1,0:T(8,128)S(1)} %bitcast.53, f32[64,16]{1,0:T(8,128)S(1)} %get-tuple-element.260), kind=kOutput, calls=%fused_computation.10.clone.1 | convolution fusion | flops 806092800 | bytes 16787456 | tf_op jit(solution)/shard_map/while/body/eval_jaxpr/ejz,ejx->ezx/dot_general | solution.py:45
  659.3 10.4 fusion.39
  669.7 12.8 %bitcast_add_fusion.2 = f32[256,64,64]{0,2,1:T(8,128)} fusion(f32[256,64,64]{0,2,1:T(8,128)} %get-tuple-element.248, f32[64,64,256]{2,1,0:T(8,128)} %fusion.39, pred[]{:T(512)S(6)} %compare.3, bf16[256,64,64]{0,2,1:T(8,128)(2,1)S(1)} %bitcast.48, f32[64,256,256]{2,1,0:T(8,128)} %fusion.38, pred[256,256]{1,0:T(8,128)(4,1)S(1)} %subtract_compare_fusion.2), kind=kOutput, calls=%fused_computation.9.clone.1 | convolution fusion | flops 560988160 | bytes 31522816 | tf_op jit(solution)/shard_map/while/body/eval_jaxpr/grs,sgc->rgc/dot_general | solution.py:56
  690.9 16.9 %fusion.38 = f32[64,256,256]{2,1,0:T(8,128)} fusion(f32[256]{0:T(256)S(1)} %get-tuple-element.236, f32[256]{0:T(256)S(1)} %get-tuple-element.237, f32[64,16]{1,0:T(8,128)S(1)} %bitcast.53, f32[64,16]{1,0:T(8,128)S(1)} %get-tuple-element.260), kind=kOutput, calls=%fused_computation.10.clone.1 | convolution fusion | flops 806092800 | bytes 16787456 | tf_op jit(solution)/shard_map/while/body/eval_jaxpr/ejz,ejx->ezx/dot_general | solution.py:45
  707.8 10.4 fusion.39
  718.2 12.8 %bitcast_add_fusion.2 = f32[256,64,64]{0,2,1:T(8,128)} fusion(f32[256,64,64]{0,2,1:T(8,128)} %get-tuple-element.248, f32[64,64,256]{2,1,0:T(8,128)} %fusion.39, pred[]{:T(512)S(6)} %compare.3, bf16[256,64,64]{0,2,1:T(8,128)(2,1)S(1)} %bitcast.48, f32[64,256,256]{2,1,0:T(8,128)} %fusion.38, pred[256,256]{1,0:T(8,128)(4,1)S(1)} %subtract_compare_fusion.2), kind=kOutput, calls=%fused_computation.9.clone.1 | convolution fusion | flops 560988160 | bytes 31522816 | tf_op jit(solution)/shard_map/while/body/eval_jaxpr/grs,sgc->rgc/dot_general | solution.py:56
  739.4 16.9 %fusion.38 = f32[64,256,256]{2,1,0:T(8,128)} fusion(f32[256]{0:T(256)S(1)} %get-tuple-element.236, f32[256]{0:T(256)S(1)} %get-tuple-element.237, f32[64,16]{1,0:T(8,128)S(1)} %bitcast.53, f32[64,16]{1,0:T(8,128)S(1)} %get-tuple-element.260), kind=kOutput, calls=%fused_computation.10.clone.1 | convolution fusion | flops 806092800 | bytes 16787456 | tf_op jit(solution)/shard_map/while/body/eval_jaxpr/ejz,ejx->ezx/dot_general | solution.py:45
  756.3 10.4 fusion.39
  766.7 12.8 %bitcast_add_fusion.2 = f32[256,64,64]{0,2,1:T(8,128)} fusion(f32[256,64,64]{0,2,1:T(8,128)} %get-tuple-element.248, f32[64,64,256]{2,1,0:T(8,128)} %fusion.39, pred[]{:T(512)S(6)} %compare.3, bf16[256,64,64]{0,2,1:T(8,128)(2,1)S(1)} %bitcast.48, f32[64,256,256]{2,1,0:T(8,128)} %fusion.38, pred[256,256]{1,0:T(8,128)(4,1)S(1)} %subtract_compare_fusion.2), kind=kOutput, calls=%fused_computation.9.clone.1 | convolution fusion | flops 560988160 | bytes 31522816 | tf_op jit(solution)/shard_map/while/body/eval_jaxpr/grs,sgc->rgc/dot_general | solution.py:56
  787.9 16.9 %fusion.38 = f32[64,256,256]{2,1,0:T(8,128)} fusion(f32[256]{0:T(256)S(1)} %get-tuple-element.236, f32[256]{0:T(256)S(1)} %get-tuple-element.237, f32[64,16]{1,0:T(8,128)S(1)} %bitcast.53, f32[64,16]{1,0:T(8,128)S(1)} %get-tuple-element.260), kind=kOutput, calls=%fused_computation.10.clone.1 | convolution fusion | flops 806092800 | bytes 16787456 | tf_op jit(solution)/shard_map/while/body/eval_jaxpr/ejz,ejx->ezx/dot_general | solution.py:45
  804.8 10.4 fusion.39
  815.2 12.8 %bitcast_add_fusion.2 = f32[256,64,64]{0,2,1:T(8,128)} fusion(f32[256,64,64]{0,2,1:T(8,128)} %get-tuple-element.248, f32[64,64,256]{2,1,0:T(8,128)} %fusion.39, pred[]{:T(512)S(6)} %compare.3, bf16[256,64,64]{0,2,1:T(8,128)(2,1)S(1)} %bitcast.48, f32[64,256,256]{2,1,0:T(8,128)} %fusion.38, pred[256,256]{1,0:T(8,128)(4,1)S(1)} %subtract_compare_fusion.2), kind=kOutput, calls=%fused_computation.9.clone.1 | convolution fusion | flops 560988160 | bytes 31522816 | tf_op jit(solution)/shard_map/while/body/eval_jaxpr/grs,sgc->rgc/dot_general | solution.py:56
  836.4 16.9 %fusion.38 = f32[64,256,256]{2,1,0:T(8,128)} fusion(f32[256]{0:T(256)S(1)} %get-tuple-element.236, f32[256]{0:T(256)S(1)} %get-tuple-element.237, f32[64,16]{1,0:T(8,128)S(1)} %bitcast.53, f32[64,16]{1,0:T(8,128)S(1)} %get-tuple-element.260), kind=kOutput, calls=%fused_computation.10.clone.1 | convolution fusion | flops 806092800 | bytes 16787456 | tf_op jit(solution)/shard_map/while/body/eval_jaxpr/ejz,ejx->ezx/dot_general | solution.py:45
  853.3 10.4 fusion.39
  863.6 12.8 %bitcast_add_fusion.2 = f32[256,64,64]{0,2,1:T(8,128)} fusion(f32[256,64,64]{0,2,1:T(8,128)} %get-tuple-element.248, f32[64,64,256]{2,1,0:T(8,128)} %fusion.39, pred[]{:T(512)S(6)} %compare.3, bf16[256,64,64]{0,2,1:T(8,128)(2,1)S(1)} %bitcast.48, f32[64,256,256]{2,1,0:T(8,128)} %fusion.38, pred[256,256]{1,0:T(8,128)(4,1)S(1)} %subtract_compare_fusion.2), kind=kOutput, calls=%fused_computation.9.clone.1 | convolution fusion | flops 560988160 | bytes 31522816 | tf_op jit(solution)/shard_map/while/body/eval_jaxpr/grs,sgc->rgc/dot_general | solution.py:56
  884.9 16.9 %fusion.38 = f32[64,256,256]{2,1,0:T(8,128)} fusion(f32[256]{0:T(256)S(1)} %get-tuple-element.236, f32[256]{0:T(256)S(1)} %get-tuple-element.237, f32[64,16]{1,0:T(8,128)S(1)} %bitcast.53, f32[64,16]{1,0:T(8,128)S(1)} %get-tuple-element.260), kind=kOutput, calls=%fused_computation.10.clone.1 | convolution fusion | flops 806092800 | bytes 16787456 | tf_op jit(solution)/shard_map/while/body/eval_jaxpr/ejz,ejx->ezx/dot_general | solution.py:45
  901.7 10.4 fusion.39
  912.1 12.8 %bitcast_add_fusion.2 = f32[256,64,64]{0,2,1:T(8,128)} fusion(f32[256,64,64]{0,2,1:T(8,128)} %get-tuple-element.248, f32[64,64,256]{2,1,0:T(8,128)} %fusion.39, pred[]{:T(512)S(6)} %compare.3, bf16[256,64,64]{0,2,1:T(8,128)(2,1)S(1)} %bitcast.48, f32[64,256,256]{2,1,0:T(8,128)} %fusion.38, pred[256,256]{1,0:T(8,128)(4,1)S(1)} %subtract_compare_fusion.2), kind=kOutput, calls=%fused_computation.9.clone.1 | convolution fusion | flops 560988160 | bytes 31522816 | tf_op jit(solution)/shard_map/while/body/eval_jaxpr/grs,sgc->rgc/dot_general | solution.py:56
  933.4 16.9 %fusion.38 = f32[64,256,256]{2,1,0:T(8,128)} fusion(f32[256]{0:T(256)S(1)} %get-tuple-element.236, f32[256]{0:T(256)S(1)} %get-tuple-element.237, f32[64,16]{1,0:T(8,128)S(1)} %bitcast.53, f32[64,16]{1,0:T(8,128)S(1)} %get-tuple-element.260), kind=kOutput, calls=%fused_computation.10.clone.1 | convolution fusion | flops 806092800 | bytes 16787456 | tf_op jit(solution)/shard_map/while/body/eval_jaxpr/ejz,ejx->ezx/dot_general | solution.py:45
  950.2 10.4 fusion.39
  960.6 12.8 %bitcast_add_fusion.2 = f32[256,64,64]{0,2,1:T(8,128)} fusion(f32[256,64,64]{0,2,1:T(8,128)} %get-tuple-element.248, f32[64,64,256]{2,1,0:T(8,128)} %fusion.39, pred[]{:T(512)S(6)} %compare.3, bf16[256,64,64]{0,2,1:T(8,128)(2,1)S(1)} %bitcast.48, f32[64,256,256]{2,1,0:T(8,128)} %fusion.38, pred[256,256]{1,0:T(8,128)(4,1)S(1)} %subtract_compare_fusion.2), kind=kOutput, calls=%fused_computation.9.clone.1 | convolution fusion | flops 560988160 | bytes 31522816 | tf_op jit(solution)/shard_map/while/body/eval_jaxpr/grs,sgc->rgc/dot_general | solution.py:56
  981.9 16.9 %fusion.38 = f32[64,256,256]{2,1,0:T(8,128)} fusion(f32[256]{0:T(256)S(1)} %get-tuple-element.236, f32[256]{0:T(256)S(1)} %get-tuple-element.237, f32[64,16]{1,0:T(8,128)S(1)} %bitcast.53, f32[64,16]{1,0:T(8,128)S(1)} %get-tuple-element.260), kind=kOutput, calls=%fused_computation.10.clone.1 | convolution fusion | flops 806092800 | bytes 16787456 | tf_op jit(solution)/shard_map/while/body/eval_jaxpr/ejz,ejx->ezx/dot_general | solution.py:45
  998.7 10.4 fusion.39
  1009.1 12.8 %bitcast_add_fusion.2 = f32[256,64,64]{0,2,1:T(8,128)} fusion(f32[256,64,64]{0,2,1:T(8,128)} %get-tuple-element.248, f32[64,64,256]{2,1,0:T(8,128)} %fusion.39, pred[]{:T(512)S(6)} %compare.3, bf16[256,64,64]{0,2,1:T(8,128)(2,1)S(1)} %bitcast.48, f32[64,256,256]{2,1,0:T(8,128)} %fusion.38, pred[256,256]{1,0:T(8,128)(4,1)S(1)} %subtract_compare_fusion.2), kind=kOutput, calls=%fused_computation.9.clone.1 | convolution fusion | flops 560988160 | bytes 31522816 | tf_op jit(solution)/shard_map/while/body/eval_jaxpr/grs,sgc->rgc/dot_general | solution.py:56
  1030.3 16.9 %fusion.38 = f32[64,256,256]{2,1,0:T(8,128)} fusion(f32[256]{0:T(256)S(1)} %get-tuple-element.236, f32[256]{0:T(256)S(1)} %get-tuple-element.237, f32[64,16]{1,0:T(8,128)S(1)} %bitcast.53, f32[64,16]{1,0:T(8,128)S(1)} %get-tuple-element.260), kind=kOutput, calls=%fused_computation.10.clone.1 | convolution fusion | flops 806092800 | bytes 16787456 | tf_op jit(solution)/shard_map/while/body/eval_jaxpr/ejz,ejx->ezx/dot_general | solution.py:45
  1047.2 10.4 fusion.39
  1057.6 12.8 %bitcast_add_fusion.2 = f32[256,64,64]{0,2,1:T(8,128)} fusion(f32[256,64,64]{0,2,1:T(8,128)} %get-tuple-element.248, f32[64,64,256]{2,1,0:T(8,128)} %fusion.39, pred[]{:T(512)S(6)} %compare.3, bf16[256,64,64]{0,2,1:T(8,128)(2,1)S(1)} %bitcast.48, f32[64,256,256]{2,1,0:T(8,128)} %fusion.38, pred[256,256]{1,0:T(8,128)(4,1)S(1)} %subtract_compare_fusion.2), kind=kOutput, calls=%fused_computation.9.clone.1 | convolution fusion | flops 560988160 | bytes 31522816 | tf_op jit(solution)/shard_map/while/body/eval_jaxpr/grs,sgc->rgc/dot_general | solution.py:56
  1078.8 16.9 %fusion.38 = f32[64,256,256]{2,1,0:T(8,128)} fusion(f32[256]{0:T(256)S(1)} %get-tuple-element.236, f32[256]{0:T(256)S(1)} %get-tuple-element.237, f32[64,16]{1,0:T(8,128)S(1)} %bitcast.53, f32[64,16]{1,0:T(8,128)S(1)} %get-tuple-element.260), kind=kOutput, calls=%fused_computation.10.clone.1 | convolution fusion | flops 806092800 | bytes 16787456 | tf_op jit(solution)/shard_map/while/body/eval_jaxpr/ejz,ejx->ezx/dot_general | solution.py:45
  1095.7 10.4 fusion.39
  1106.1 12.8 %bitcast_add_fusion.2 = f32[256,64,64]{0,2,1:T(8,128)} fusion(f32[256,64,64]{0,2,1:T(8,128)} %get-tuple-element.248, f32[64,64,256]{2,1,0:T(8,128)} %fusion.39, pred[]{:T(512)S(6)} %compare.3, bf16[256,64,64]{0,2,1:T(8,128)(2,1)S(1)} %bitcast.48, f32[64,256,256]{2,1,0:T(8,128)} %fusion.38, pred[256,256]{1,0:T(8,128)(4,1)S(1)} %subtract_compare_fusion.2), kind=kOutput, calls=%fused_computation.9.clone.1 | convolution fusion | flops 560988160 | bytes 31522816 | tf_op jit(solution)/shard_map/while/body/eval_jaxpr/grs,sgc->rgc/dot_general | solution.py:56
  1118.9 4.6 convert_convert_fusion
  1123.5 5.8 reshape.112
  1129.3 7.3 copy.46
  1136.6 4.0 multiply_convert_fusion
  1140.6 27.3 %all_to_all.34 = bf16[2,128,4096]{2,1,0:T(8,128)(2,1)S(1)} all-to-all(bf16[2,128,4096]{2,1,0:T(8,128)(2,1)S(1)} %multiply_convert_fusion), channel_id=1, replica_groups=mesh['ctx'=16,'mp'=2] {'mp'}, dimensions={0} | all-to-all | bytes 4194304 | tf_op jit(solution)/shard_map/all_to_all | solution.py:109
  1170.3 4.1 copy.48
  (126 shorter events, 144.6 us)
Async XLA Ops:
  6.5 20.2 %copy-start.2 = (s32[32]{0:T(128)S(1)}, s32[32]{0:T(128)}, u32[]{:S(2)}) copy-start(s32[32]{0:T(128)} %param.11) | copy-start | bytes 388
  19.7 99.6 %all-to-all-start = ((bf16[128,3,8192]{0,1,2:T(4,128)(2,1)}), bf16[128,3,8192]{0,1,2:T(4,128)(2,1)}, u32[]{:S(2)}, u32[]{:S(2)}) async-start(bf16[128,3,8192]{0,1,2:T(4,128)(2,1)} %copy.38), calls=%async_computation | async-start | bytes 16777216 | tf_op jit(solution)/shard_map/all_to_all | solution.py:89
  26.6 317.7 %all-gather.3.cloned.1.call-start = ((), (), s32[]{:S(2)}) async-start(), calls=%async_computation.2 | async-start | bytes 35651584 | tf_op jit(solution)/shard_map/all_gather | solution.py:74
  136.0 7.1 collective-permute-start
  171.1 3.6 copy-start
  171.1 3.7 copy-start.1
Sparse Core Ops, SparseCore 0:
  174.8 169.4 all-gather.2
where the time goes:
time: 1190 us; the launch traced here: 1180 us
  matrix products  640 us (54%)
  waiting for transfers between devices  260 us (22%)
  local copies, waits for them, and re-layouts  165 us (14%)
  other arithmetic  63.2 us (5%)
  blocking collectives  27.3 us (2%)
  between operations  13.5 us (1%)
    dot_general x16, matrix products, filter_tile(): jnp.einsum('ejz,ejx->ezx', left_neighbor, right_neighbor, precision=lax.P...  270 us
    dot_general x16, matrix products, split_product(): jnp.einsum(form, lower_part, inputs, preferred_element_type=jnp.float32)  204 us
    all_gather x1, waiting for transfers between devices, long_filter(): piece_rows = lax.all_gather(product, 'ctx', axis=0, tiled=True)  169 us
    dot_general x16, matrix products, split_product(): jnp.einsum(form, upper_part, inputs, preferred_element_type=jnp.float32)  166 us
    dynamic_slice x48, local copies, waits for them, and re-layouts, long_filter(): result, unused = lax.scan(scan_step, initial, (stacked, starts))  112 us
    all_to_all x1, waiting for transfers between devices, shards(): lax.all_to_all(proj, 'mp', split_axis=2, concat_axis=0, tiled=True)  88.5 us
    add x1, other arithmetic, short_convolution(): result + conv_weight[:, position_shift, :][None] * earlier * keep_mask.as...  27.9 us
    all_to_all x1, blocking collectives, shards(): lax.all_to_all(mixed_out, 'mp', split_axis=0, concat_axis=1, tiled=True)  27.3 us
  transfers between devices with their start and end apart: 3, of which 3 were waited for; matrix products, arithmetic and copies ran while one was open for 0% of the time, Pallas kernels for 0%

commit v1 on v0

v1 whole, which is shorter than its diff:
```python
import functools

import jax
import jax.numpy as jnp
from jax import lax
from jax.experimental import pallas as pl
from jax.experimental.pallas import tpu as pltpu
from jax.sharding import PartitionSpec as P

LANES = 128
HALO = 8
AXES = ("ctx", "mp")
F32 = jnp.float32
BF16 = jnp.bfloat16


def rows_since_start(doc_lengths, positions):
    order = jnp.arange(doc_lengths.shape[0])
    ahead = order[None, :] < order[:, None]
    starts = jnp.sum(jnp.where(ahead, doc_lengths[None, :], 0), axis=1)
    begun = starts[None, :] <= positions[:, None]
    return positions - jnp.max(jnp.where(begun, starts[None, :], 0), axis=1)


def lag_lanes(rows):
    return lax.broadcasted_iota(jnp.int32, (rows, LANES), 1)


def conv_tile(window, x_ref, halo_ref, w_ref, mask_ref, j, columns):
    taps, rows = w_ref.shape[1], x_ref.shape[1]
    window[:HALO] = halo_ref[j, :, columns].astype(F32)
    window[HALO:] = x_ref[j, :, columns].astype(F32)
    total = w_ref[j, 0:1, columns] * window[HALO:]
    for k in range(1, taps):
        earlier = window[HALO - k : HALO - k + rows] * mask_ref[k]
        total = total + w_ref[j, k : k + 1, columns] * earlier
    return total


def group_rows(ref, group, modes):
    return ref[group * modes : (group + 1) * modes]


def state_kernel(modes, x_ref, halo_ref, w_ref, mask_ref, decay_ref, u_ref, state_ref, win_k, win_v):
    rows = x_ref.shape[1]
    left = lag_lanes(modes) < LANES // 2
    ages = (rows - 1 - lag_lanes(modes)).astype(F32)
    for tile in range(x_ref.shape[2] // LANES):
        columns = slice(tile * LANES, (tile + 1) * LANES)
        keys = conv_tile(win_k, x_ref, halo_ref, w_ref, mask_ref, 0, columns)
        values = conv_tile(win_v, x_ref, halo_ref, w_ref, mask_ref, 1, columns)
        u = (keys * values).astype(BF16)
        u_ref[:, columns] = u
        halves = []
        for side in range(2):
            decay = group_rows(decay_ref, 2 * tile + side, modes)
            weight = jnp.exp(-decay * ages).astype(BF16)[:, :rows]
            halves.append(jnp.dot(weight, u, preferred_element_type=F32))
        state_ref[:, columns] = jnp.where(left, halves[0], halves[1]).astype(BF16)


def prefix_kernel(rows, r_ref, decay_ref, p_ref):
    devices = r_ref.shape[0]
    step = jnp.exp(-decay_ref[...] * float(rows))

    def body(j, carry):
        p_ref[j] = carry.astype(BF16)
        return step * carry + r_ref[j].astype(F32)

    lax.fori_loop(0, devices, body, jnp.zeros(r_ref.shape[1:], F32))


def mix_kernel(modes, x_ref, halo_ref, w_ref, mask_ref, decay_ref, coef_ref, u_ref, carry_ref, o_ref, win_q):
    rows = x_ref.shape[1]
    left = lag_lanes(rows) < LANES // 2
    lane = lag_lanes(modes)
    after = (lane + 1).astype(F32)
    back = jnp.where(lane == 0, 0, LANES - lane).astype(F32)
    causal = lag_lanes(rows) <= lax.broadcasted_iota(jnp.int32, (rows, LANES), 0)
    for tile in range(x_ref.shape[2] // LANES):
        columns = slice(tile * LANES, (tile + 1) * LANES)
        query = conv_tile(win_q, x_ref, halo_ref, w_ref, mask_ref, 0, columns)
        u = u_ref[:, columns]
        carry = carry_ref[:, columns]
        halves = []
        for side in range(2):
            decay = group_rows(decay_ref, 2 * tile + side, modes)
            coef = group_rows(coef_ref, 2 * tile + side, modes)
            into = (coef * jnp.exp(-decay * after)).astype(BF16)[:, :rows]
            taps = jnp.sum(coef * jnp.exp(-decay * back), axis=0, keepdims=True)
            spread = pltpu.roll(jnp.broadcast_to(taps, (rows, LANES)), 0, 1, stride=1, stride_axis=0)
            local = jnp.where(causal, spread, 0.0).astype(BF16)[:, :rows]
            half = jnp.dot(local, u, preferred_element_type=F32)
            half += lax.dot_general(into, carry, (((0,), (0,)), ((), ())), preferred_element_type=F32)
            halves.append(half)
        z = jnp.where(left, halves[0], halves[1]).astype(BF16).astype(F32)
        o_ref[:, columns] = (query * z).astype(BF16)


def everywhere(block, axis):
    n = lax.axis_size(axis)
    copies = jnp.broadcast_to(block[None], (n,) + block.shape)
    return lax.all_to_all(copies, axis, 0, 0, tiled=True).reshape((-1,) + block.shape[1:])


def shards(proj, conv_weight, residues, decays, doc_lengths):
    rows, _, width = proj.shape
    taps = conv_weight.shape[1]
    modes = residues.shape[1]
    devices = lax.axis_size("ctx") * lax.axis_size("mp")
    me = lax.axis_index("ctx") * lax.axis_size("mp") + lax.axis_index("mp")

    x = proj.transpose(1, 0, 2)
    halo = lax.ppermute(x[:, rows - HALO :], AXES, [(i, i + 1) for i in range(devices - 1)])
    both = everywhere(jnp.concatenate([residues, decays], axis=1), "mp")
    residues, decays = both[:, :modes], both[:, modes:]
    groups = residues.shape[0]
    coef = (residues * jnp.sqrt(decays)).reshape(-1, 1)
    coef = jnp.broadcast_to(coef, (groups * modes, LANES))
    decay = jnp.broadcast_to(decays.reshape(-1, 1), (groups * modes, LANES))
    since = rows_since_start(doc_lengths, me * rows + jnp.arange(rows, dtype=jnp.int32))
    mask = (since[None, :] >= jnp.arange(taps)[:, None]).astype(F32)
    mask = jnp.broadcast_to(mask[:, :, None], (taps, rows, LANES))

    block = 512
    per = modes * groups * block // width
    row_block = lambda n: pl.BlockSpec((n, block), lambda i: (0, i))
    whole_mask = pl.BlockSpec(mask.shape, lambda i: (0, 0, 0))
    mode_block = pl.BlockSpec((per, LANES), lambda i: (i, 0))
    window = pltpu.VMEM((rows + HALO, LANES), F32)
    params = pltpu.CompilerParams(vmem_limit_bytes=48 * 2**20)

    def three(n, a, j):
        return pl.BlockSpec((a, n, block), lambda i: (j, 0, i))

    u, state = pl.pallas_call(
        functools.partial(state_kernel, modes),
        grid=(width // block,),
        out_shape=(jax.ShapeDtypeStruct((rows, width), BF16), jax.ShapeDtypeStruct((modes, width), BF16)),
        in_specs=[three(rows, 2, 0), three(HALO, 2, 0), three(taps, 2, 0), whole_mask, mode_block],
        out_specs=(row_block(rows), row_block(modes)),
        scratch_shapes=[window, window],
        compiler_params=params,
    )(x[1:], halo[1:], conv_weight[1:], mask, decay)

    share = width // devices
    sent = state.reshape(modes, devices, share).transpose(1, 0, 2)
    received = lax.all_to_all(sent, AXES, 0, 0, tiled=True)
    channel = me * share + jnp.arange(share, dtype=jnp.int32)
    my_decay = jnp.take(decays, channel // (width // groups), axis=0).T
    before = pl.pallas_call(
        functools.partial(prefix_kernel, rows),
        out_shape=jax.ShapeDtypeStruct((devices, modes, share), BF16),
        compiler_params=params,
    )(received, my_decay)
    carry = lax.all_to_all(before, AXES, 0, 0, tiled=True)
    carry = carry.transpose(1, 0, 2).reshape(modes, width)

    return pl.pallas_call(
        functools.partial(mix_kernel, modes),
        grid=(width // block,),
        out_shape=jax.ShapeDtypeStruct((rows, width), BF16),
        in_specs=[
            three(rows, 1, 0),
            three(HALO, 1, 0),
            three(taps, 1, 0),
            whole_mask,
            mode_block,
            mode_block,
            row_block(rows),
            row_block(modes),
        ],
        out_specs=row_block(rows),
        scratch_shapes=[window],
        compiler_params=params,
    )(x, halo, conv_weight, mask, decay, coef, u, carry)


def solution(mesh):
    return jax.shard_map(
        shards,
        mesh=mesh,
        in_specs=(P(AXES, None, None), P(), P("mp", None), P("mp", None), P()),
        out_specs=P(AXES, None),
        check_vma=False,
    )
```

time: 1190 us -> 81.6 us (0.07)
  matrix products: 640 us -> 0 us
  waiting for transfers between devices: 260 us -> 22.5 us
  local copies, waits for them, and re-layouts: 165 us -> 12.5 us
  other arithmetic: 63.2 us -> 2.43 us
  blocking collectives: 27.3 us -> 0 us
  Pallas kernels: 0 us -> 26.2 us
  between operations: 13.5 us -> 0.17 us
    dot_general x48 -> x0, matrix products: 640 us -> none  [the longest x16 270 us: filter_tile(): jnp.einsum('ejz,ejx->ezx', left_neighbor, right_neighbor, precision=lax.P...]
    all_gather x1 -> x0, waiting for transfers between devices: 169 us -> none  [long_filter(): piece_rows = lax.all_gather(product, 'ctx', axis=0, tiled=True)]
    dynamic_slice x48 -> x0, local copies, waits for them, and re-layouts: 112 us -> none  [long_filter(): result, unused = lax.scan(scan_step, initial, (stacked, starts))]
    all_to_all x1 -> x3, waiting for transfers between devices: 88.5 us -> 20.3 us  [the longest x1 10.6 us: shards(): carry = lax.all_to_all(before, AXES, 0, 0, tiled=True)]
    add x2 -> x1, other arithmetic: 28 us -> 0.01 us  [shards(): me * rows + jnp.arange(rows, dtype=jnp.int32)]
    all_to_all x1 -> x0, blocking collectives: 27.3 us -> none  [shards(): lax.all_to_all(mixed_out, 'mp', split_axis=0, concat_axis=1, tiled=True)]
    pallas_call x0 -> x3, Pallas kernels: none -> 26.2 us  [the longest x1 12.8 us: shards(): pl.pallas_call(functools.partial(state_kernel, modes), grid=(width // blo...]
    all_to_all x4 -> x2, local copies, waits for them, and re-layouts: 22.2 us -> 0.6 us  [everywhere(): lax.all_to_all(copies, axis, 0, 0, tiled=True)]
  transfers between devices with their start and end apart: 3 -> 4, of which waited for: 3 -> 3; matrix products, arithmetic and copies ran while one was open for 0% -> 11% of each run, Pallas kernels for 0% -> 0%
where the time goes in v1:
time: 81.6 us; the launch traced here: 80.3 us
  Pallas kernels  26.2 us (32%)
  waiting for transfers between devices  22.5 us (28%)
  starting transfers between devices  16.5 us (20%)
  local copies, waits for them, and re-layouts  12.5 us (15%)
  other arithmetic  2.43 us (3%)
    pallas_call x1, Pallas kernels, shards(): pl.pallas_call(functools.partial(state_kernel, modes), grid=(width // blo...  12.8 us
    pallas_call x1, Pallas kernels, shards(): pl.pallas_call(functools.partial(mix_kernel, modes), grid=(width // block...  12.5 us
    all_to_all x1, waiting for transfers between devices, shards(): carry = lax.all_to_all(before, AXES, 0, 0, tiled=True)  10.6 us
    all_to_all x1, waiting for transfers between devices, shards(): received = lax.all_to_all(sent, AXES, 0, 0, tiled=True)  9.69 us
    all_to_all x1, starting transfers between devices, shards(): received = lax.all_to_all(sent, AXES, 0, 0, tiled=True)  6.7 us
    slice x1, local copies, waits for them, and re-layouts, shards(): x[1:]  4.64 us
    ppermute x1, starting transfers between devices, shards(): lax.ppermute(x[:, rows - HALO:], AXES, [(i, i + 1) for i in range(devices...  3.88 us
    unnamed x9, local copies, waits for them, and re-layouts  3.7 us
  transfers between devices with their start and end apart: 4, of which 3 were waited for; matrix products, arithmetic and copies ran while one was open for 11% of the time, Pallas kernels for 0%

profile of v1, /device:TPU:1, one launch (start us, length us, event | category | flops | bytes accessed | tf_op | source)
XLA Modules:
  0.0 80.3 jit_solution(16098416305162391233)
XLA Ops:
  0.0 0.7 pad_maximum_fusion
  0.7 0.7 reshape.124
  1.4 3.3 %all-to-all-start = ((f32[2,1,2048]{2,1,0:T(1,128)}), f32[2,1,2048]{2,1,0:T(1,128)S(1)}, u32[]{:S(2)}, u32[]{:S(2)}) async-start(f32[2,1,2048]{2,1,0:T(1,128)} %reshape.124), calls=%async_computation | async-start | bytes 32768 | tf_op jit(solution)/shard_map/all_to_all | solution.py:103
  4.7 1.0 %slice.26 = bf16[3,8,8192]{2,1,0:T(8,128)(2,1)S(1)} slice(bf16[3,128,8192]{2,1,0:T(8,128)(2,1)} %bitcast.20), slice={[0:3], [120:128], [0:8192]} | slice | bytes 786432 | tf_op jit(solution)/shard_map/slice | solution.py:114
  5.8 3.9 %collective-permute-start = (bf16[3,8,8192]{2,1,0:T(8,128)(2,1)S(1)}, bf16[3,8,8192]{2,1,0:T(8,128)(2,1)S(1)}, u32[]{:S(2)}, u32[]{:S(2)}) collective-permute-start(bf16[3,8,8192]{2,1,0:T(8,128)(2,1)S(1)} %slice.26), channel_id=1, source_target_pairs={{0,1},{1,2},{2,3},{3,4},{4,5},{5,6},{6,7},{7,8},{8,9},{9,10},{10,1... | collective-permute-start | bytes 1179656 | tf_op jit(solution)/shard_map/ppermute | solution.py:114
  9.7 0.8 select_reduce_fusion.1
  10.4 0.1 select_reduce_fusion
  10.6 0.0 copy-start
  10.6 4.6 %slice.29.x_ref = bf16[2,128,8192]{2,1,0:T(8,128)(2,1)} slice(bf16[3,128,8192]{2,1,0:T(8,128)(2,1)} %bitcast.21), slice={[1:3], [0:128], [0:8192]} | slice | bytes 8388608 | tf_op jit(solution)/shard_map/slice | solution.py:144
  15.2 0.0 copy-done
  15.2 0.0 all-to-all-done
  15.3 0.5 broadcast.133
  15.8 0.7 reduce
  16.5 0.1 reshape.125
  16.6 0.1 copy.17
  16.6 0.1 slice_multiply_fusion
  16.8 0.1 broadcast_in_dim.71
  16.8 2.2 %collective-permute-done.halo_ref = bf16[3,8,8192]{2,1,0:T(8,128)(2,1)S(1)} collective-permute-done((bf16[3,8,8192]{2,1,0:T(8,128)(2,1)S(1)}, bf16[3,8,8192]{2,1,0:T(8,128)(2,1)S(1)}, u32[]{:S(2)}, u32[]{:S(2)}) %collective-permute-start) | collective-permute-done | bytes 393248 | tf_op jit(solution)/shard_map/ppermute | solution.py:114
  19.1 0.2 broadcast_in_dim.69.mask_ref
  19.3 0.3 broadcast_in_dim.72.decay_ref
  19.6 12.8 %shard_map.55 = (bf16[128,8192]{1,0:T(8,128)(2,1)S(1)}, bf16[16,8192]{1,0:T(8,128)(2,1)S(1)}) custom-call(bf16[2,128,8192]{2,1,0:T(8,128)(2,1)} %slice.29.x_ref, bf16[2,8,8192]{2,1,0:T(8,128)(2,1)S(1)} %slice.30.halo_ref, f32[2,7,8192]{2,1,0:T(8,128)S(1)} %slice.23.w_ref, f32[7,128,128]{2,1,0:T(8,128)S(1)} %broadcast_in_dim.69.mask_ref, ...), custom_call_target="tpu_custom_call" | custom-call | tf_op jit(solution)/shard_map/pallas_call | solution.py:136
  32.4 0.0 copy-start.1
  32.4 1.3 %copy-done.1 = bf16[128,8192]{1,0:T(8,128)(2,1)} copy-done((bf16[128,8192]{1,0:T(8,128)(2,1)}, bf16[128,8192]{1,0:T(8,128)(2,1)S(1)}, u32[]{:S(2)}) %copy-start.1) | copy-done | bytes 2097176
  33.7 0.7 copy.24
  34.4 6.7 %all-to-all-start.1 = ((bf16[32,16,256]{2,1,0:T(8,128)(2,1)}), bf16[32,16,256]{2,1,0:T(8,128)(2,1)S(1)}, u32[]{:S(2)}, u32[]{:S(2)}) async-start(bf16[32,16,256]{2,1,0:T(8,128)(2,1)} %bitcast.17), calls=%async_computation.1 | async-start | bytes 524288 | tf_op jit(solution)/shard_map/all_to_all | solution.py:148
  41.2 0.7 gather_fusion
  41.9 0.1 copy.19
  42.0 9.7 %all-to-all-done.1.r_ref = bf16[32,16,256]{2,1,0:T(8,128)(2,1)S(1)} async-done(((bf16[32,16,256]{2,1,0:T(8,128)(2,1)}), bf16[32,16,256]{2,1,0:T(8,128)(2,1)S(1)}, u32[]{:S(2)}, u32[]{:S(2)}) %all-to-all-start.1) | async-done | bytes 262176 | tf_op jit(solution)/shard_map/all_to_all | solution.py:148
  51.6 0.9 %shard_map.56 = bf16[32,16,256]{2,1,0:T(8,128)(2,1)} custom-call(bf16[32,16,256]{2,1,0:T(8,128)(2,1)S(1)} %all-to-all-done.1.r_ref, f32[16,256]{1,0:T(8,128)S(1)} %select_bitcast_fusion.decay_ref), custom_call_target="tpu_custom_call" | custom-call | tf_op jit(solution)/shard_map/pallas_call | solution.py:151
  52.5 2.6 %all-to-all-start.2 = ((bf16[32,16,256]{2,1,0:T(8,128)(2,1)}), bf16[32,16,256]{2,1,0:T(8,128)(2,1)S(1)}, u32[]{:S(2)}, u32[]{:S(2)}) async-start(bf16[32,16,256]{2,1,0:T(8,128)(2,1)} %shard_map.56), calls=%async_computation.2 | async-start | bytes 524288 | tf_op jit(solution)/shard_map/all_to_all | solution.py:156
  55.1 0.1 broadcast_in_dim.73
  55.2 10.6 %all-to-all-done.2 = bf16[32,16,256]{2,1,0:T(8,128)(2,1)S(1)} async-done(((bf16[32,16,256]{2,1,0:T(8,128)(2,1)}), bf16[32,16,256]{2,1,0:T(8,128)(2,1)S(1)}, u32[]{:S(2)}, u32[]{:S(2)}) %all-to-all-start.2) | async-done | bytes 262176 | tf_op jit(solution)/shard_map/all_to_all | solution.py:156
  65.8 0.3 broadcast_in_dim.74.coef_ref
  66.2 0.0 copy-start.2
  66.2 1.6 %copy-done.2 = bf16[128,8192]{1,0:T(8,128)(2,1)S(1)} copy-done((bf16[128,8192]{1,0:T(8,128)(2,1)S(1)}, bf16[128,8192]{1,0:T(8,128)(2,1)}, u32[]{:S(2)}) %copy-start.2) | copy-done | bytes 2097176
  67.8 12.5 %shard_map.57 = bf16[128,8192]{1,0:T(8,128)(2,1)} custom-call(bf16[3,128,8192]{2,1,0:T(8,128)(2,1)} %bitcast.22, bf16[3,8,8192]{2,1,0:T(8,128)(2,1)S(1)} %collective-permute-done.halo_ref, f32[3,7,8192]{2,1,0:T(8,128)S(1)} %copy-done, f32[7,128,128]{2,1,0:T(8,128)S(1)} %broadcast_in_dim.69.mask_ref, f32[2048,128]{1,0:T(8,128)S(1)} %broadcast_in_dim.72.decay_ref, ...), custom_call_target="tpu_custom_call" | custom-call | tf_op jit(solution)/shard_map/pallas_call | solution.py:159
  (11 shorter events, 0.1 us)
Async XLA Ops:
  1.4 13.8 %all-to-all-start = ((f32[2,1,2048]{2,1,0:T(1,128)}), f32[2,1,2048]{2,1,0:T(1,128)S(1)}, u32[]{:S(2)}, u32[]{:S(2)}) async-start(f32[2,1,2048]{2,1,0:T(1,128)} %reshape.124), calls=%async_computation | async-start | bytes 32768 | tf_op jit(solution)/shard_map/all_to_all | solution.py:103
  5.8 13.3 %collective-permute-start = (bf16[3,8,8192]{2,1,0:T(8,128)(2,1)S(1)}, bf16[3,8,8192]{2,1,0:T(8,128)(2,1)S(1)}, u32[]{:S(2)}, u32[]{:S(2)}) collective-permute-start(bf16[3,8,8192]{2,1,0:T(8,128)(2,1)S(1)} %slice.26), channel_id=1, source_target_pairs={{0,1},{1,2},{2,3},{3,4},{4,5},{5,6},{6,7},{7,8},{8,9},{9,10},{10,1... | collective-permute-start | bytes 1179656 | tf_op jit(solution)/shard_map/ppermute | solution.py:114
  10.6 4.7 %copy-start = (f32[3,7,8192]{2,1,0:T(8,128)S(1)}, f32[3,7,8192]{2,1,0:T(8,128)}, u32[]{:S(2)}) copy-start(f32[3,7,8192]{2,1,0:T(8,128)} %w_ref.1) | copy-start | bytes 2064388
  32.4 1.3 %copy-start.1 = (bf16[128,8192]{1,0:T(8,128)(2,1)}, bf16[128,8192]{1,0:T(8,128)(2,1)S(1)}, u32[]{:S(2)}) copy-start(bf16[128,8192]{1,0:T(8,128)(2,1)S(1)} %get-tuple-element.7.u_ref) | copy-start | bytes 6291460
  34.4 17.3 %all-to-all-start.1 = ((bf16[32,16,256]{2,1,0:T(8,128)(2,1)}), bf16[32,16,256]{2,1,0:T(8,128)(2,1)S(1)}, u32[]{:S(2)}, u32[]{:S(2)}) async-start(bf16[32,16,256]{2,1,0:T(8,128)(2,1)} %bitcast.17), calls=%async_computation.1 | async-start | bytes 524288 | tf_op jit(solution)/shard_map/all_to_all | solution.py:148
  52.5 13.3 %all-to-all-start.2 = ((bf16[32,16,256]{2,1,0:T(8,128)(2,1)}), bf16[32,16,256]{2,1,0:T(8,128)(2,1)S(1)}, u32[]{:S(2)}, u32[]{:S(2)}) async-start(bf16[32,16,256]{2,1,0:T(8,128)(2,1)} %shard_map.56), calls=%async_computation.2 | async-start | bytes 524288 | tf_op jit(solution)/shard_map/all_to_all | solution.py:156
  66.2 1.6 %copy-start.2 = (bf16[128,8192]{1,0:T(8,128)(2,1)S(1)}, bf16[128,8192]{1,0:T(8,128)(2,1)}, u32[]{:S(2)}) copy-start(bf16[128,8192]{1,0:T(8,128)(2,1)} %copy-done.1) | copy-start | bytes 6291460

commit v2 on v1

v2 whole, which is shorter than its diff:
```python
import functools

import jax
import jax.numpy as jnp
from jax import lax
from jax.experimental import pallas as pl
from jax.experimental.pallas import tpu as pltpu
from jax.sharding import PartitionSpec as P

LANES = 128
HALO = 8
UNROLL = 2
AXES = ("ctx", "mp")
F32 = jnp.float32
BF16 = jnp.bfloat16


def rows_since_start(doc_lengths, positions):
    order = jnp.arange(doc_lengths.shape[0])
    ahead = order[None, :] < order[:, None]
    starts = jnp.sum(jnp.where(ahead, doc_lengths[None, :], 0), axis=1)
    begun = starts[None, :] <= positions[:, None]
    return positions - jnp.max(jnp.where(begun, starts[None, :], 0), axis=1)


def lag_lanes(rows):
    return lax.broadcasted_iota(jnp.int32, (rows, LANES), 1)


def conv_tiles(windows, x_ref, halo_ref, w_ref, mask_ref, parts, columns):
    taps, rows = w_ref.shape[1], x_ref.shape[1]
    chunk = min(rows, 64)
    for window, j in zip(windows, parts):
        window[:HALO] = halo_ref[j, :, columns].astype(F32)
        window[HALO:] = x_ref[j, :, columns].astype(F32)
    pieces = [[] for _ in parts]
    for first in range(0, rows, chunk):
        totals = [
            w_ref[j, 0:1, columns] * window[HALO + first : HALO + first + chunk]
            for window, j in zip(windows, parts)
        ]
        for k in range(1, taps):
            keep = mask_ref[k, first : first + chunk]
            start = HALO - k + first
            for i, j in enumerate(parts):
                earlier = windows[i][start : start + chunk] * keep
                totals[i] = totals[i] + w_ref[j, k : k + 1, columns] * earlier
        for i, total in enumerate(totals):
            pieces[i].append(total)
    return [jnp.concatenate(p, axis=0) for p in pieces]


def mixer_kernel(
    sizes,
    x_ref,
    halo_ref,
    w_ref,
    mask_ref,
    decay_ref,
    coef_ref,
    my_decay_ref,
    o_ref,
    u_ref,
    y_ref,
    q_ref,
    state_ref,
    carry_ref,
    seen_ref,
    before_ref,
    wins,
    local_sem,
    send_sems,
    recv_sems,
):
    modes, devices, mp, share, stride = sizes
    rows, width = x_ref.shape[1:]
    owners = width // share
    me = lax.axis_index("ctx") * mp + lax.axis_index("mp")
    tiles = width // LANES
    pair = 2 * modes

    def peer(i):
        other = lax.rem(me + i, devices)
        return other, (other // mp, lax.rem(other, mp))

    barrier = pltpu.get_barrier_semaphore()

    @pl.loop(1, devices)
    def _(i):
        pl.semaphore_signal(barrier, inc=1, device_id=peer(i)[1], device_id_type=pl.DeviceIdType.MESH)

    left = lag_lanes(modes) < LANES // 2
    lane = lag_lanes(pair)
    ages = (rows - 1 - lane).astype(F32)

    def cols(tile):
        return pl.ds(pl.multiple_of(tile * LANES, LANES), LANES)

    def mode_rows(ref, tile):
        return ref[pl.ds(pl.multiple_of(tile * pair, pair), pair)]

    @pl.loop(0, tiles // UNROLL)
    def _(step):
        for part in range(UNROLL):
            tile = step * UNROLL + part
            columns = cols(tile)
            two = [wins.at[2 * part], wins.at[2 * part + 1]]
            keys, values = conv_tiles(two, x_ref, halo_ref, w_ref, mask_ref, (1, 2), columns)
            u = (keys * values).astype(BF16)
            u_ref[:, columns] = u
            weight = jnp.exp(-mode_rows(decay_ref, tile) * ages).astype(BF16)[:, :rows]
            sums = jnp.dot(weight, u, preferred_element_type=F32)
            state_ref[:, columns] = jnp.where(left, sums[:modes], sums[modes:]).astype(BF16)

    pl.semaphore_wait(barrier, devices - 1)

    def share_of(index):
        return pl.ds(pl.multiple_of(index * share, share), share)

    def is_owner(index):
        return lax.rem(index, stride) == 0

    def when(always, condition):
        return (lambda f: f()) if always else pl.when(condition)

    @pl.loop(1, devices)
    def _(i):
        other, where = peer(i)

        @when(stride == 1, is_owner(other))
        def _():
            pltpu.make_async_remote_copy(
                state_ref.at[:, share_of(other // stride)],
                seen_ref.at[me],
                send_sems.at[0],
                recv_sems.at[0],
                device_id=where,
                device_id_type=pl.DeviceIdType.MESH,
            ).start()

    @when(stride == 1, is_owner(me))
    def _():
        own = pltpu.make_async_copy(state_ref.at[:, share_of(me // stride)], seen_ref.at[me], local_sem)
        own.start()
        own.wait()

    wide_left = lag_lanes(rows) < LANES // 2
    back = jnp.where(lane == 0, 0, LANES - lane).astype(F32)
    causal = lag_lanes(rows) <= lax.broadcasted_iota(jnp.int32, (rows, LANES), 0)

    @pl.loop(0, tiles // UNROLL)
    def _(step):
        for part in range(UNROLL):
            tile = step * UNROLL + part
            columns = cols(tile)
            (query,) = conv_tiles([wins.at[2 * part]], x_ref, halo_ref, w_ref, mask_ref, (0,), columns)
            q_ref[:, columns] = query
            u = u_ref[:, columns]
            terms = mode_rows(coef_ref, tile) * jnp.exp(-mode_rows(decay_ref, tile) * back)
            halves = []
            for side in range(2):
                taps = jnp.sum(terms[side * modes : (side + 1) * modes], axis=0, keepdims=True)
                spread = pltpu.roll(jnp.broadcast_to(taps, (rows, LANES)), 0, 1, stride=1, stride_axis=0)
                local = jnp.where(causal, spread, 0.0).astype(BF16)[:, :rows]
                halves.append(jnp.dot(local, u, preferred_element_type=F32))
            y_ref[:, columns] = jnp.where(wide_left, halves[0], halves[1])

    @when(stride == 1, is_owner(me))
    def _():
        others = seen_ref.at[pl.ds(0, devices - 1)]
        pltpu.make_async_copy(others, others, recv_sems.at[0]).wait()
        decayed = jnp.exp(-my_decay_ref[...] * float(rows))

        def body(j, carry):
            before_ref[j] = carry.astype(BF16)
            return decayed * carry + seen_ref[j].astype(F32)

        lax.fori_loop(0, devices, body, jnp.zeros(seen_ref.shape[1:], F32))

        @pl.loop(1, devices)
        def _(i):
            other, where = peer(i)
            pltpu.make_async_remote_copy(
                before_ref.at[other],
                carry_ref.at[:, share_of(me // stride)],
                send_sems.at[1],
                recv_sems.at[1],
                device_id=where,
                device_id_type=pl.DeviceIdType.MESH,
            ).start()

        own = pltpu.make_async_copy(before_ref.at[me], carry_ref.at[:, share_of(me // stride)], local_sem)
        own.start()
        own.wait()

    def wait_shares(sem, count):
        some = carry_ref.at[:, pl.ds(0, count * share)]
        pltpu.make_async_copy(some, some, sem).wait()

    if stride == 1:
        wait_shares(send_sems.at[0], owners - 1)
        wait_shares(recv_sems.at[1], owners - 1)
    else:

        @pl.when(is_owner(me))
        def _():
            wait_shares(send_sems.at[0], owners - 1)
            wait_shares(recv_sems.at[1], owners - 1)

        @pl.when(jnp.logical_not(is_owner(me)))
        def _():
            wait_shares(send_sems.at[0], owners)
            wait_shares(recv_sems.at[1], owners)

    after = (lane + 1).astype(F32)
    @pl.loop(0, tiles // UNROLL)
    def _(step):
        for part in range(UNROLL):
            tile = step * UNROLL + part
            columns = cols(tile)
            into = (mode_rows(coef_ref, tile) * jnp.exp(-mode_rows(decay_ref, tile) * after)).astype(BF16)[:, :rows]
            carry = carry_ref[:, columns].astype(F32)
            split = jnp.concatenate([jnp.where(left, carry, 0.0), jnp.where(left, 0.0, carry)], axis=0)
            gained = lax.dot_general(into, split.astype(BF16), (((0,), (0,)), ((), ())), preferred_element_type=F32)
            z = (y_ref[:, columns] + gained).astype(BF16).astype(F32)
            o_ref[:, columns] = (q_ref[:, columns] * z).astype(BF16)

    @when(stride == 1, is_owner(me))
    def _():
        others = before_ref.at[pl.ds(0, devices - 1)]
        pltpu.make_async_copy(others, others, send_sems.at[1]).wait()


def everywhere(block, axis):
    n = lax.axis_size(axis)
    copies = jnp.broadcast_to(block[None], (n,) + block.shape)
    return lax.all_to_all(copies, axis, 0, 0, tiled=True).reshape((-1,) + block.shape[1:])


def shards(proj, conv_weight, residues, decays, doc_lengths):
    rows, _, width = proj.shape
    taps = conv_weight.shape[1]
    modes = residues.shape[1]
    devices = lax.axis_size("ctx") * lax.axis_size("mp")
    me = lax.axis_index("ctx") * lax.axis_size("mp") + lax.axis_index("mp")

    x = proj.transpose(1, 0, 2)
    halo = lax.ppermute(x[:, rows - HALO :], AXES, [(i, i + 1) for i in range(devices - 1)])
    both = everywhere(jnp.concatenate([residues, decays], axis=1), "mp")
    residues, decays = both[:, :modes], both[:, modes:]
    groups = residues.shape[0]
    coef = (residues * jnp.sqrt(decays)).reshape(-1, 1)
    coef = jnp.broadcast_to(coef, (groups * modes, LANES))
    decay = jnp.broadcast_to(decays.reshape(-1, 1), (groups * modes, LANES))
    since = rows_since_start(doc_lengths, me * rows + jnp.arange(rows, dtype=jnp.int32))
    mask = (since[None, :] >= jnp.arange(taps)[:, None]).astype(F32)
    mask = jnp.broadcast_to(mask[:, :, None], (taps, rows, LANES))

    mp = lax.axis_size("mp")
    share = max(width // devices, LANES)
    stride = devices * share // width
    channel = (me // stride) * share + jnp.arange(share, dtype=jnp.int32)
    my_decay = jnp.take(decays, channel // (width // groups), axis=0).T
    in_vmem = pl.BlockSpec(memory_space=pltpu.VMEM)
    return pl.pallas_call(
        functools.partial(mixer_kernel, (modes, devices, mp, share, stride)),
        out_shape=jax.ShapeDtypeStruct((rows, width), BF16),
        in_specs=[in_vmem] * 7,
        out_specs=in_vmem,
        scratch_shapes=[
            pltpu.VMEM((rows, width), BF16),
            pltpu.VMEM((rows, width), F32),
            pltpu.VMEM((rows, width), F32),
            pltpu.VMEM((modes, width), BF16),
            pltpu.VMEM((modes, width), BF16),
            pltpu.VMEM((devices, modes, share), BF16),
            pltpu.VMEM((devices, modes, share), BF16),
            pltpu.VMEM((2 * UNROLL, rows + HALO, LANES), F32),
            pltpu.SemaphoreType.DMA,
            pltpu.SemaphoreType.DMA((2,)),
            pltpu.SemaphoreType.DMA((2,)),
        ],
        compiler_params=pltpu.CompilerParams(
            collective_id=0, has_side_effects=True, vmem_limit_bytes=48 * 2**20
        ),
    )(x, halo, conv_weight, mask, decay, coef, my_decay)


def solution(mesh):
    return jax.shard_map(
        shards,
        mesh=mesh,
        in_specs=(P(AXES, None, None), P(), P("mp", None), P("mp", None), P()),
        out_specs=P(AXES, None),
        check_vma=False,
    )
```

time: 81.6 us -> 61.7 us (0.76); the launches traced: 80.3 us -> 61.3 us
  waiting for transfers between devices: 22.5 us -> 5.99 us
  Pallas kernels: 26.2 us -> 40 us
  starting transfers between devices: 16.5 us -> 7.19 us
  local copies, waits for them, and re-layouts: 12.5 us -> 5.52 us
    all_to_all x2 -> x0, waiting for transfers between devices: 20.3 us -> none  [the longest x1 10.6 us: shards(): carry = lax.all_to_all(before, AXES, 0, 0, tiled=True)]
    pallas_call x3 -> x1, Pallas kernels: 26.2 us -> 40 us  [shards(): pl.pallas_call(functools.partial(mixer_kernel, (modes, devices, mp, share...]
    all_to_all x2 -> x0, starting transfers between devices: 9.28 us -> none  [the longest x1 6.7 us: shards(): received = lax.all_to_all(sent, AXES, 0, 0, tiled=True)]
    slice x3 -> x0, local copies, waits for them, and re-layouts: 4.7 us -> none  [the longest x1 4.64 us: shards(): x[1:]]
    ppermute x1, waiting for transfers between devices: 2.24 us -> 5.99 us  [shards(): lax.ppermute(x[:, rows - HALO:], AXES, [(i, i + 1) for i in range(devices...]
    unnamed x9 -> x6, local copies, waits for them, and re-layouts: 3.7 us -> 2.12 us
  transfers between devices with their start and end apart: 4 -> 2, of which waited for: 3 -> 1; matrix products, arithmetic and copies ran while one was open for 11% -> 7% of each run, Pallas kernels for 0% -> 0%
where the time goes in v2:
time: 61.7 us; the launch traced here: 61.3 us
  Pallas kernels  40 us (65%)
  starting transfers between devices  7.19 us (12%)
  waiting for transfers between devices  5.99 us (10%)
  local copies, waits for them, and re-layouts  5.52 us (9%)
  other arithmetic  2.43 us (4%)
    pallas_call x1, Pallas kernels, shards(): pl.pallas_call(functools.partial(mixer_kernel, (modes, devices, mp, share...  40 us
    ppermute x1, waiting for transfers between devices, shards(): lax.ppermute(x[:, rows - HALO:], AXES, [(i, i + 1) for i in range(devices...  5.99 us
    ppermute x1, starting transfers between devices, shards(): lax.ppermute(x[:, rows - HALO:], AXES, [(i, i + 1) for i in range(devices...  3.88 us
    all_to_all x1, starting transfers between devices, everywhere(): lax.all_to_all(copies, axis, 0, 0, tiled=True)  3.31 us
    unnamed x6, local copies, waits for them, and re-layouts  2.12 us
  transfers between devices with their start and end apart: 2, of which 1 were waited for; matrix products, arithmetic and copies ran while one was open for 7% of the time, Pallas kernels for 0%

profile of v2, /device:TPU:1, one launch (start us, length us, event | category | flops | bytes accessed | tf_op | source)
XLA Modules:
  0.0 61.3 jit_solution(4030903105917409703)
XLA Ops:
  0.0 0.7 %pad_maximum_fusion = f32[64,32]{0,1:T(8,128)S(1)} fusion(f32[64,16]{0,1:T(8,128)} %param.8, f32[64,16]{0,1:T(8,128)} %param.7), kind=kLoop, calls=%fused_computation.2 | loop fusion | flops 2048 | bytes 16384 | tf_op jit(solution)/shard_map/concatenate | solution.py:249
  0.7 0.7 %reshape.116 = f32[2,1,2048]{2,1,0:T(1,128)} reshape(f32[2,32,64]{2,1,0:T(8,128)S(1)} %broadcast_bitcast_fusion) | data formatting | bytes 32768
  1.4 3.3 %all-to-all-start = ((f32[2,1,2048]{2,1,0:T(1,128)}), f32[2,1,2048]{2,1,0:T(1,128)S(1)}, u32[]{:S(2)}, u32[]{:S(2)}) async-start(f32[2,1,2048]{2,1,0:T(1,128)} %reshape.116), calls=%async_computation | async-start | bytes 32768 | tf_op jit(solution)/shard_map/all_to_all | solution.py:237
  4.7 1.0 %slice.14 = bf16[3,8,8192]{2,1,0:T(8,128)(2,1)S(1)} slice(bf16[3,128,8192]{2,1,0:T(8,128)(2,1)} %bitcast.8), slice={[0:3], [120:128], [0:8192]} | slice | bytes 786432 | tf_op jit(solution)/shard_map/slice | solution.py:248
  5.8 3.9 %collective-permute-start = (bf16[3,8,8192]{2,1,0:T(8,128)(2,1)S(1)}, bf16[3,8,8192]{2,1,0:T(8,128)(2,1)S(1)}, u32[]{:S(2)}, u32[]{:S(2)}) collective-permute-start(bf16[3,8,8192]{2,1,0:T(8,128)(2,1)S(1)} %slice.14), channel_id=1, source_target_pairs={{0,1},{1,2},{2,3},{3,4},{4,5},{5,6},{6,7},{7,8},{8,9},{9,10},{10,1... | collective-permute-start | bytes 1179656 | tf_op jit(solution)/shard_map/ppermute | solution.py:248
  9.7 0.8 %select_reduce_fusion.1 = s32[32]{0:T(128)S(1)} fusion(s32[32]{0:T(128)} %param.9), kind=kLoop, calls=%fused_computation.5 | loop fusion | flops 3040 | bytes 256 | tf_op jit(solution)/shard_map/reduce_sum | solution.py:21
  10.4 0.1 select_reduce_fusion
  10.6 0.0 all-to-all-done
  10.6 0.5 broadcast.142
  11.1 0.7 %reduce = f32[2,2048]{1,0:T(2,128)S(1)} reduce(f32[2,1,2048]{2,1,0:T(1,128)S(1)} %all-to-all-done, f32[]{:T(128)} %broadcast.142), dimensions={1}, to_apply=%all_to_all.3.reduce_sub_computation | reduce | bytes 32772 | tf_op jit(solution)/shard_map/all_to_all | solution.py:237
  11.8 0.1 reshape.117
  11.9 0.1 copy.12
  12.0 0.1 slice_multiply_fusion
  12.1 0.0 copy-start
  12.1 0.1 broadcast_in_dim.73
  12.2 0.1 broadcast_in_dim.71
  12.3 0.7 %gather_fusion = f32[256,16]{1,0:T(8,128)S(1)} fusion(f32[128,16]{1,0:T(8,128)S(1)} %get-tuple-element.6, s32[1024]{0:T(1024)S(1)} %pad_clamp_fusion), kind=kCustom, calls=%fused_computation | custom fusion | bytes 33792 | tf_op jit(solution)/shard_map/jit(_take)/gather | solution.py:263
  13.0 0.1 copy.13
  13.1 6.0 %collective-permute-done.halo_ref = bf16[3,8,8192]{2,1,0:T(8,128)(2,1)S(1)} collective-permute-done((bf16[3,8,8192]{2,1,0:T(8,128)(2,1)S(1)}, bf16[3,8,8192]{2,1,0:T(8,128)(2,1)S(1)}, u32[]{:S(2)}, u32[]{:S(2)}) %collective-permute-start) | collective-permute-done | bytes 393248 | tf_op jit(solution)/shard_map/ppermute | solution.py:248
  19.1 0.2 broadcast_in_dim.69.mask_ref
  19.3 0.3 broadcast_in_dim.72.decay_ref
  19.6 0.3 broadcast_in_dim.74.coef_ref
  19.9 0.0 copy-done
  19.9 40.0 %shard_map.55 = bf16[128,8192]{1,0:T(8,128)(2,1)S(1)} custom-call(bf16[3,128,8192]{2,1,0:T(8,128)(2,1)} %bitcast.9, bf16[3,8,8192]{2,1,0:T(8,128)(2,1)S(1)} %collective-permute-done.halo_ref, f32[3,7,8192]{2,1,0:T(8,128)S(1)} %copy-done, f32[7,128,128]{2,1,0:T(8,128)S(1)} %broadcast_in_dim.69.mask_ref, f32[2048,128]{1,0:T(8,128)S(1)} %broadcast_in_dim.72.decay_ref, ...), custom_call_target="tpu_custom_call" | custom-call | tf_op jit(solution)/shard_map/pallas_call | solution.py:265
  60.0 1.3 %copy.15 = bf16[128,8192]{1,0:T(8,128)(2,1)} copy(bf16[128,8192]{1,0:T(8,128)(2,1)S(1)} %shard_map.55) | data formatting | bytes 4194304
  (8 shorter events, 0.1 us)
Async XLA Ops:
  1.4 9.2 %all-to-all-start = ((f32[2,1,2048]{2,1,0:T(1,128)}), f32[2,1,2048]{2,1,0:T(1,128)S(1)}, u32[]{:S(2)}, u32[]{:S(2)}) async-start(f32[2,1,2048]{2,1,0:T(1,128)} %reshape.116), calls=%async_computation | async-start | bytes 32768 | tf_op jit(solution)/shard_map/all_to_all | solution.py:237
  5.8 13.3 %collective-permute-start = (bf16[3,8,8192]{2,1,0:T(8,128)(2,1)S(1)}, bf16[3,8,8192]{2,1,0:T(8,128)(2,1)S(1)}, u32[]{:S(2)}, u32[]{:S(2)}) collective-permute-start(bf16[3,8,8192]{2,1,0:T(8,128)(2,1)S(1)} %slice.14), channel_id=1, source_target_pairs={{0,1},{1,2},{2,3},{3,4},{4,5},{5,6},{6,7},{7,8},{8,9},{9,10},{10,1... | collective-permute-start | bytes 1179656 | tf_op jit(solution)/shard_map/ppermute | solution.py:248
  12.1 7.8 %copy-start = (f32[3,7,8192]{2,1,0:T(8,128)S(1)}, f32[3,7,8192]{2,1,0:T(8,128)}, u32[]{:S(2)}) copy-start(f32[3,7,8192]{2,1,0:T(8,128)} %w_ref.1) | copy-start | bytes 2064388

commit v3 on v2

--- a/solution.py
+++ b/solution.py
@@ -9,7 +9,7 @@
 
 LANES = 128
 HALO = 8
-UNROLL = 2
+UNROLL = 4
 AXES = ("ctx", "mp")
 F32 = jnp.float32
 BF16 = jnp.bfloat16
@@ -233,8 +233,14 @@
 
 def everywhere(block, axis):
     n = lax.axis_size(axis)
-    copies = jnp.broadcast_to(block[None], (n,) + block.shape)
-    return lax.all_to_all(copies, axis, 0, 0, tiled=True).reshape((-1,) + block.shape[1:])
+    me = lax.axis_index(axis)
+    gathered = jnp.zeros((n,) + block.shape, block.dtype)
+    gathered = lax.dynamic_update_index_in_dim(gathered, block, me, 0)
+    for shift in range(1, n):
+        arrived = lax.ppermute(block, axis, [(i, (i + shift) % n) for i in range(n)])
+        source = lax.rem(me - shift + n, n)
+        gathered = lax.dynamic_update_index_in_dim(gathered, arrived, source, 0)
+    return gathered.reshape((-1,) + block.shape[1:])
 
 
 def shards(proj, conv_weight, residues, decays, doc_lengths):

time: 61.7 us -> 52.7 us (0.85)
  Pallas kernels: 40 us -> 33.2 us
  starting transfers between devices: 7.19 us -> 3.96 us
  waiting for transfers between devices: 5.99 us -> 7.87 us
  other arithmetic: 2.43 us -> 1.02 us
    pallas_call x1, Pallas kernels: 40 us -> 33.2 us  [shards(): pl.pallas_call(functools.partial(mixer_kernel, (modes, devices, mp, share...]
    all_to_all x1 -> x0, starting transfers between devices: 3.31 us -> none  [everywhere(): lax.all_to_all(copies, axis, 0, 0, tiled=True)]
    ppermute x0 -> x1, starting transfers between devices: none -> 2.04 us  [everywhere(): lax.ppermute(block, axis, [(i, (i + shift) % n) for i in range(n)])]
    ppermute x1, starting transfers between devices: 3.88 us -> 1.92 us  [shards(): lax.ppermute(x[:, rows - HALO:], AXES, [(i, i + 1) for i in range(devices...]
    ppermute x1, waiting for transfers between devices: 5.99 us -> 7.87 us  [shards(): lax.ppermute(x[:, rows - HALO:], AXES, [(i, i + 1) for i in range(devices...]
    concatenate x1 -> x0, other arithmetic: 0.72 us -> none  [shards(): both = everywhere(jnp.concatenate([residues, decays], axis=1), 'mp')]
    concatenate x0 -> x1, local copies, waits for them, and re-layouts: none -> 0.7 us  [shards(): both = everywhere(jnp.concatenate([residues, decays], axis=1), 'mp')]
    all_to_all x1 -> x0, other arithmetic: 0.69 us -> none  [everywhere(): lax.all_to_all(copies, axis, 0, 0, tiled=True)]
  transfers between devices with their start and end apart: 2 -> 2, of which waited for: 1 -> 1; matrix products, arithmetic and copies ran while one was open for 7% -> 6% of each run, Pallas kernels for 0% -> 0%
where the time goes in v3:
time: 52.7 us; the launch traced here: 51.9 us
  Pallas kernels  33.2 us (63%)
  waiting for transfers between devices  7.87 us (15%)
  local copies, waits for them, and re-layouts  5.71 us (11%)
  starting transfers between devices  3.96 us (8%)
  other arithmetic  1.02 us (2%)
    pallas_call x1, Pallas kernels, shards(): pl.pallas_call(functools.partial(mixer_kernel, (modes, devices, mp, share...  33.2 us
    ppermute x1, waiting for transfers between devices, shards(): lax.ppermute(x[:, rows - HALO:], AXES, [(i, i + 1) for i in range(devices...  7.87 us
    ppermute x1, starting transfers between devices, everywhere(): lax.ppermute(block, axis, [(i, (i + shift) % n) for i in range(n)])  2.04 us
    unnamed x4, local copies, waits for them, and re-layouts  2.03 us
    ppermute x1, starting transfers between devices, shards(): lax.ppermute(x[:, rows - HALO:], AXES, [(i, i + 1) for i in range(devices...  1.92 us
  transfers between devices with their start and end apart: 2, of which 1 were waited for; matrix products, arithmetic and copies ran while one was open for 6% of the time, Pallas kernels for 0%

profile of v3, /device:TPU:1, one launch (start us, length us, event | category | flops | bytes accessed | tf_op | source)
XLA Modules:
  0.0 51.9 jit_solution(8861855618463845688)
XLA Ops:
  0.0 0.7 %constant_dynamic-update-slice_fusion.1 = f32[64,32]{0,1:T(8,128)S(1)} fusion(f32[64,16]{0,1:T(8,128)} %param.7), kind=kLoop, calls=%fused_computation.9 | loop fusion | bytes 12288
  0.7 0.7 %constant_dynamic-update-slice_fusion = f32[64,32]{0,1:T(8,128)S(1)} fusion(f32[64,32]{0,1:T(8,128)S(1)} %constant_dynamic-update-slice_fusion.1, f32[64,16]{0,1:T(8,128)} %param.8), kind=kLoop, calls=%fused_computation.8 | loop fusion | bytes 12288 | tf_op jit(solution)/shard_map/concatenate | solution.py:255
  1.4 2.0 %collective-permute-start.1 = (f32[64,32]{0,1:T(8,128)S(1)}, f32[64,32]{0,1:T(8,128)S(1)}, u32[]{:S(2)}, u32[]{:S(2)}) collective-permute-start(f32[64,32]{0,1:T(8,128)S(1)} %constant_dynamic-update-slice_fusion), channel_id=1, source_target_pairs={{0,1},{1,0},{2,3},{3,2},{4,5},{5,4},{6,7},{7,6},{8,9},{9,8},{10,11... | collective-permute-start | bytes 24584 | tf_op jit(solution)/shard_map/ppermute | solution.py:240
  3.4 1.0 %slice.14 = bf16[3,8,8192]{2,1,0:T(8,128)(2,1)S(1)} slice(bf16[3,128,8192]{2,1,0:T(8,128)(2,1)} %bitcast.7), slice={[0:3], [120:128], [0:8192]} | slice | bytes 786432 | tf_op jit(solution)/shard_map/slice | solution.py:254
  4.5 1.9 %collective-permute-start = (bf16[3,8,8192]{2,1,0:T(8,128)(2,1)S(1)}, bf16[3,8,8192]{2,1,0:T(8,128)(2,1)S(1)}, u32[]{:S(2)}, u32[]{:S(2)}) collective-permute-start(bf16[3,8,8192]{2,1,0:T(8,128)(2,1)S(1)} %slice.14), channel_id=1, source_target_pairs={{0,1},{1,2},{2,3},{3,4},{4,5},{5,6},{6,7},{7,8},{8,9},{9,10},{10,1... | collective-permute-start | bytes 1179656 | tf_op jit(solution)/shard_map/ppermute | solution.py:254
  6.4 0.8 %select_reduce_fusion.1 = s32[32]{0:T(128)S(1)} fusion(s32[32]{0:T(128)} %param.9), kind=kLoop, calls=%fused_computation.4 | loop fusion | flops 3040 | bytes 256 | tf_op jit(solution)/shard_map/reduce_sum | solution.py:21
  7.2 0.1 select_reduce_fusion
  7.3 0.1 copy.12
  7.5 0.0 collective-permute-done.1
  7.5 0.1 copy.13
  7.6 0.1 slice_multiply_fusion
  7.7 0.0 copy-start
  7.7 0.1 broadcast_in_dim.79
  7.8 0.1 broadcast_in_dim.77
  7.8 0.7 %gather_fusion = f32[256,16]{1,0:T(8,128)S(1)} fusion(f32[128,16]{1,0:T(8,128)S(1)} %get-tuple-element.6, s32[1024]{0:T(1024)S(1)} %pad_clamp_fusion), kind=kCustom, calls=%fused_computation | custom fusion | bytes 33792 | tf_op jit(solution)/shard_map/jit(_take)/gather | solution.py:269
  8.6 0.1 copy.14
  8.7 7.9 %collective-permute-done.halo_ref = bf16[3,8,8192]{2,1,0:T(8,128)(2,1)S(1)} collective-permute-done((bf16[3,8,8192]{2,1,0:T(8,128)(2,1)S(1)}, bf16[3,8,8192]{2,1,0:T(8,128)(2,1)S(1)}, u32[]{:S(2)}, u32[]{:S(2)}) %collective-permute-start) | collective-permute-done | bytes 393248 | tf_op jit(solution)/shard_map/ppermute | solution.py:254
  16.5 0.2 broadcast_in_dim.73.mask_ref
  16.7 0.3 broadcast_in_dim.78.decay_ref
  17.0 0.3 broadcast_in_dim.80.coef_ref
  17.4 0.0 copy-done
  17.4 33.2 %shard_map.55 = bf16[128,8192]{1,0:T(8,128)(2,1)S(1)} custom-call(bf16[3,128,8192]{2,1,0:T(8,128)(2,1)} %bitcast.8, bf16[3,8,8192]{2,1,0:T(8,128)(2,1)S(1)} %collective-permute-done.halo_ref, f32[3,7,8192]{2,1,0:T(8,128)S(1)} %copy-done, f32[7,128,128]{2,1,0:T(8,128)S(1)} %broadcast_in_dim.73.mask_ref, f32[2048,128]{1,0:T(8,128)S(1)} %broadcast_in_dim.78.decay_ref, ...), custom_call_target="tpu_custom_call" | custom-call | tf_op jit(solution)/shard_map/pallas_call | solution.py:271
  50.6 1.3 %copy.19 = bf16[128,8192]{1,0:T(8,128)(2,1)} copy(bf16[128,8192]{1,0:T(8,128)(2,1)S(1)} %shard_map.55) | data formatting | bytes 4194304
  (10 shorter events, 0.1 us)
Async XLA Ops:
  1.4 6.1 %collective-permute-start.1 = (f32[64,32]{0,1:T(8,128)S(1)}, f32[64,32]{0,1:T(8,128)S(1)}, u32[]{:S(2)}, u32[]{:S(2)}) collective-permute-start(f32[64,32]{0,1:T(8,128)S(1)} %constant_dynamic-update-slice_fusion), channel_id=1, source_target_pairs={{0,1},{1,0},{2,3},{3,2},{4,5},{5,4},{6,7},{7,6},{8,9},{9,8},{10,11... | collective-permute-start | bytes 24584 | tf_op jit(solution)/shard_map/ppermute | solution.py:240
  4.5 12.1 %collective-permute-start = (bf16[3,8,8192]{2,1,0:T(8,128)(2,1)S(1)}, bf16[3,8,8192]{2,1,0:T(8,128)(2,1)S(1)}, u32[]{:S(2)}, u32[]{:S(2)}) collective-permute-start(bf16[3,8,8192]{2,1,0:T(8,128)(2,1)S(1)} %slice.14), channel_id=1, source_target_pairs={{0,1},{1,2},{2,3},{3,4},{4,5},{5,6},{6,7},{7,8},{8,9},{9,10},{10,1... | collective-permute-start | bytes 1179656 | tf_op jit(solution)/shard_map/ppermute | solution.py:254
  7.7 9.7 %copy-start = (f32[3,7,8192]{2,1,0:T(8,128)S(1)}, f32[3,7,8192]{2,1,0:T(8,128)}, u32[]{:S(2)}) copy-start(f32[3,7,8192]{2,1,0:T(8,128)} %w_ref.1) | copy-start | bytes 2064388

commit v4 on v3

--- a/solution.py
+++ b/solution.py
@@ -9,7 +9,7 @@
 
 LANES = 128
 HALO = 8
-UNROLL = 4
+UNROLL = 8
 AXES = ("ctx", "mp")
 F32 = jnp.float32
 BF16 = jnp.bfloat16

time: 52.7 us -> 50.1 us (0.951)
  Pallas kernels: 33.2 us -> 30.6 us
    pallas_call x1, Pallas kernels: 33.2 us -> 30.6 us  [shards(): pl.pallas_call(functools.partial(mixer_kernel, (modes, devices, mp, share...]
where the time goes in v4:
time: 50.1 us; the launch traced here: 49.3 us
  Pallas kernels  30.6 us (61%)
  waiting for transfers between devices  7.87 us (16%)
  local copies, waits for them, and re-layouts  5.71 us (11%)
  starting transfers between devices  3.96 us (8%)
  other arithmetic  1.02 us (2%)
    pallas_call x1, Pallas kernels, shards(): pl.pallas_call(functools.partial(mixer_kernel, (modes, devices, mp, share...  30.6 us
    ppermute x1, waiting for transfers between devices, shards(): lax.ppermute(x[:, rows - HALO:], AXES, [(i, i + 1) for i in range(devices...  7.87 us
    ppermute x1, starting transfers between devices, everywhere(): lax.ppermute(block, axis, [(i, (i + shift) % n) for i in range(n)])  2.04 us
    unnamed x4, local copies, waits for them, and re-layouts  2.03 us
    ppermute x1, starting transfers between devices, shards(): lax.ppermute(x[:, rows - HALO:], AXES, [(i, i + 1) for i in range(devices...  1.92 us
    slice x1, local copies, waits for them, and re-layouts, shards(): x[:, rows - HALO:]  1.02 us
  transfers between devices with their start and end apart: 2, of which 1 were waited for; matrix products, arithmetic and copies ran while one was open for 6% of the time, Pallas kernels for 0%

profile of v4, /device:TPU:1, one launch (start us, length us, event | category | flops | bytes accessed | tf_op | source)
XLA Modules:
  0.0 49.3 jit_solution(7264317337727738797)
XLA Ops:
  0.0 0.7 %constant_dynamic-update-slice_fusion.1 = f32[64,32]{0,1:T(8,128)S(1)} fusion(f32[64,16]{0,1:T(8,128)} %param.7), kind=kLoop, calls=%fused_computation.9 | loop fusion | bytes 12288
  0.7 0.7 %constant_dynamic-update-slice_fusion = f32[64,32]{0,1:T(8,128)S(1)} fusion(f32[64,32]{0,1:T(8,128)S(1)} %constant_dynamic-update-slice_fusion.1, f32[64,16]{0,1:T(8,128)} %param.8), kind=kLoop, calls=%fused_computation.8 | loop fusion | bytes 12288 | tf_op jit(solution)/shard_map/concatenate | solution.py:255
  1.4 2.0 %collective-permute-start.1 = (f32[64,32]{0,1:T(8,128)S(1)}, f32[64,32]{0,1:T(8,128)S(1)}, u32[]{:S(2)}, u32[]{:S(2)}) collective-permute-start(f32[64,32]{0,1:T(8,128)S(1)} %constant_dynamic-update-slice_fusion), channel_id=1, source_target_pairs={{0,1},{1,0},{2,3},{3,2},{4,5},{5,4},{6,7},{7,6},{8,9},{9,8},{10,11... | collective-permute-start | bytes 24584 | tf_op jit(solution)/shard_map/ppermute | solution.py:240
  3.4 1.0 %slice.14 = bf16[3,8,8192]{2,1,0:T(8,128)(2,1)S(1)} slice(bf16[3,128,8192]{2,1,0:T(8,128)(2,1)} %bitcast.7), slice={[0:3], [120:128], [0:8192]} | slice | bytes 786432 | tf_op jit(solution)/shard_map/slice | solution.py:254
  4.5 1.9 %collective-permute-start = (bf16[3,8,8192]{2,1,0:T(8,128)(2,1)S(1)}, bf16[3,8,8192]{2,1,0:T(8,128)(2,1)S(1)}, u32[]{:S(2)}, u32[]{:S(2)}) collective-permute-start(bf16[3,8,8192]{2,1,0:T(8,128)(2,1)S(1)} %slice.14), channel_id=1, source_target_pairs={{0,1},{1,2},{2,3},{3,4},{4,5},{5,6},{6,7},{7,8},{8,9},{9,10},{10,1... | collective-permute-start | bytes 1179656 | tf_op jit(solution)/shard_map/ppermute | solution.py:254
  6.4 0.8 %select_reduce_fusion.1 = s32[32]{0:T(128)S(1)} fusion(s32[32]{0:T(128)} %param.9), kind=kLoop, calls=%fused_computation.4 | loop fusion | flops 3040 | bytes 256 | tf_op jit(solution)/shard_map/reduce_sum | solution.py:21
  7.2 0.1 select_reduce_fusion
  7.3 0.1 copy.12
  7.5 0.0 collective-permute-done.1
  7.5 0.1 copy.13
  7.6 0.1 slice_multiply_fusion
  7.7 0.0 copy-start
  7.7 0.1 broadcast_in_dim.79
  7.8 0.1 broadcast_in_dim.77
  7.8 0.7 %gather_fusion = f32[256,16]{1,0:T(8,128)S(1)} fusion(f32[128,16]{1,0:T(8,128)S(1)} %get-tuple-element.6, s32[1024]{0:T(1024)S(1)} %pad_clamp_fusion), kind=kCustom, calls=%fused_computation | custom fusion | bytes 33792 | tf_op jit(solution)/shard_map/jit(_take)/gather | solution.py:269
  8.6 0.1 copy.14
  8.7 7.9 %collective-permute-done.halo_ref = bf16[3,8,8192]{2,1,0:T(8,128)(2,1)S(1)} collective-permute-done((bf16[3,8,8192]{2,1,0:T(8,128)(2,1)S(1)}, bf16[3,8,8192]{2,1,0:T(8,128)(2,1)S(1)}, u32[]{:S(2)}, u32[]{:S(2)}) %collective-permute-start) | collective-permute-done | bytes 393248 | tf_op jit(solution)/shard_map/ppermute | solution.py:254
  16.5 0.2 broadcast_in_dim.73.mask_ref
  16.7 0.3 broadcast_in_dim.78.decay_ref
  17.0 0.3 broadcast_in_dim.80.coef_ref
  17.4 0.0 copy-done
  17.4 30.6 %shard_map.55 = bf16[128,8192]{1,0:T(8,128)(2,1)S(1)} custom-call(bf16[3,128,8192]{2,1,0:T(8,128)(2,1)} %bitcast.8, bf16[3,8,8192]{2,1,0:T(8,128)(2,1)S(1)} %collective-permute-done.halo_ref, f32[3,7,8192]{2,1,0:T(8,128)S(1)} %copy-done, f32[7,128,128]{2,1,0:T(8,128)S(1)} %broadcast_in_dim.73.mask_ref, f32[2048,128]{1,0:T(8,128)S(1)} %broadcast_in_dim.78.decay_ref, ...), custom_call_target="tpu_custom_call" | custom-call | tf_op jit(solution)/shard_map/pallas_call | solution.py:271
  48.0 1.3 %copy.19 = bf16[128,8192]{1,0:T(8,128)(2,1)} copy(bf16[128,8192]{1,0:T(8,128)(2,1)S(1)} %shard_map.55) | data formatting | bytes 4194304
  (10 shorter events, 0.1 us)
Async XLA Ops:
  1.4 6.1 %collective-permute-start.1 = (f32[64,32]{0,1:T(8,128)S(1)}, f32[64,32]{0,1:T(8,128)S(1)}, u32[]{:S(2)}, u32[]{:S(2)}) collective-permute-start(f32[64,32]{0,1:T(8,128)S(1)} %constant_dynamic-update-slice_fusion), channel_id=1, source_target_pairs={{0,1},{1,0},{2,3},{3,2},{4,5},{5,4},{6,7},{7,6},{8,9},{9,8},{10,11... | collective-permute-start | bytes 24584 | tf_op jit(solution)/shard_map/ppermute | solution.py:240
  4.5 12.1 %collective-permute-start = (bf16[3,8,8192]{2,1,0:T(8,128)(2,1)S(1)}, bf16[3,8,8192]{2,1,0:T(8,128)(2,1)S(1)}, u32[]{:S(2)}, u32[]{:S(2)}) collective-permute-start(bf16[3,8,8192]{2,1,0:T(8,128)(2,1)S(1)} %slice.14), channel_id=1, source_target_pairs={{0,1},{1,2},{2,3},{3,4},{4,5},{5,6},{6,7},{7,8},{8,9},{9,10},{10,1... | collective-permute-start | bytes 1179656 | tf_op jit(solution)/shard_map/ppermute | solution.py:254
  7.7 9.7 %copy-start = (f32[3,7,8192]{2,1,0:T(8,128)S(1)}, f32[3,7,8192]{2,1,0:T(8,128)}, u32[]{:S(2)}) copy-start(f32[3,7,8192]{2,1,0:T(8,128)} %w_ref.1) | copy-start | bytes 2064388

commit v5 on v4

--- a/solution.py
+++ b/solution.py
@@ -148,8 +148,7 @@
     back = jnp.where(lane == 0, 0, LANES - lane).astype(F32)
     causal = lag_lanes(rows) <= lax.broadcasted_iota(jnp.int32, (rows, LANES), 0)
 
-    @pl.loop(0, tiles // UNROLL)
-    def _(step):
+    def local_step(step):
         for part in range(UNROLL):
             tile = step * UNROLL + part
             columns = cols(tile)
@@ -165,6 +164,9 @@
                 halves.append(jnp.dot(local, u, preferred_element_type=F32))
             y_ref[:, columns] = jnp.where(wide_left, halves[0], halves[1])
 
+    steps = tiles // UNROLL
+    pl.loop(0, steps // 2)(local_step)
+
     @when(stride == 1, is_owner(me))
     def _():
         others = seen_ref.at[pl.ds(0, devices - 1)]
@@ -192,6 +194,8 @@
         own = pltpu.make_async_copy(before_ref.at[me], carry_ref.at[:, share_of(me // stride)], local_sem)
         own.start()
         own.wait()
+
+    pl.loop(steps // 2, steps)(local_step)
 
     def wait_shares(sem, count):
         some = carry_ref.at[:, pl.ds(0, count * share)]

time: 50.1 us -> 50.1 us (level)
  no operation moved by 1% of the time
where the time goes in v5:
time: 50.1 us; the launch traced here: 49.3 us
  Pallas kernels  30.6 us (61%)
  waiting for transfers between devices  7.87 us (16%)
  local copies, waits for them, and re-layouts  5.71 us (11%)
  starting transfers between devices  3.96 us (8%)
  other arithmetic  1.02 us (2%)
    pallas_call x1, Pallas kernels, shards(): pl.pallas_call(functools.partial(mixer_kernel, (modes, devices, mp, share...  30.6 us
    ppermute x1, waiting for transfers between devices, shards(): lax.ppermute(x[:, rows - HALO:], AXES, [(i, i + 1) for i in range(devices...  7.87 us
    ppermute x1, starting transfers between devices, everywhere(): lax.ppermute(block, axis, [(i, (i + shift) % n) for i in range(n)])  2.04 us
    unnamed x4, local copies, waits for them, and re-layouts  2.03 us
    ppermute x1, starting transfers between devices, shards(): lax.ppermute(x[:, rows - HALO:], AXES, [(i, i + 1) for i in range(devices...  1.92 us
    slice x1, local copies, waits for them, and re-layouts, shards(): x[:, rows - HALO:]  1.02 us
  transfers between devices with their start and end apart: 2, of which 1 were waited for; matrix products, arithmetic and copies ran while one was open for 6% of the time, Pallas kernels for 0%

profile of v5, /device:TPU:1, one launch (start us, length us, event | category | flops | bytes accessed | tf_op | source)
XLA Modules:
  0.0 49.3 jit_solution(7119941191244231661)
XLA Ops:
  0.0 0.7 %constant_dynamic-update-slice_fusion.1 = f32[64,32]{0,1:T(8,128)S(1)} fusion(f32[64,16]{0,1:T(8,128)} %param.7), kind=kLoop, calls=%fused_computation.9 | loop fusion | bytes 12288
  0.7 0.7 %constant_dynamic-update-slice_fusion = f32[64,32]{0,1:T(8,128)S(1)} fusion(f32[64,32]{0,1:T(8,128)S(1)} %constant_dynamic-update-slice_fusion.1, f32[64,16]{0,1:T(8,128)} %param.8), kind=kLoop, calls=%fused_computation.8 | loop fusion | bytes 12288 | tf_op jit(solution)/shard_map/concatenate | solution.py:259
  1.4 2.0 %collective-permute-start.1 = (f32[64,32]{0,1:T(8,128)S(1)}, f32[64,32]{0,1:T(8,128)S(1)}, u32[]{:S(2)}, u32[]{:S(2)}) collective-permute-start(f32[64,32]{0,1:T(8,128)S(1)} %constant_dynamic-update-slice_fusion), channel_id=1, source_target_pairs={{0,1},{1,0},{2,3},{3,2},{4,5},{5,4},{6,7},{7,6},{8,9},{9,8},{10,11... | collective-permute-start | bytes 24584 | tf_op jit(solution)/shard_map/ppermute | solution.py:244
  3.4 1.0 %slice.14 = bf16[3,8,8192]{2,1,0:T(8,128)(2,1)S(1)} slice(bf16[3,128,8192]{2,1,0:T(8,128)(2,1)} %bitcast.7), slice={[0:3], [120:128], [0:8192]} | slice | bytes 786432 | tf_op jit(solution)/shard_map/slice | solution.py:258
  4.5 1.9 %collective-permute-start = (bf16[3,8,8192]{2,1,0:T(8,128)(2,1)S(1)}, bf16[3,8,8192]{2,1,0:T(8,128)(2,1)S(1)}, u32[]{:S(2)}, u32[]{:S(2)}) collective-permute-start(bf16[3,8,8192]{2,1,0:T(8,128)(2,1)S(1)} %slice.14), channel_id=1, source_target_pairs={{0,1},{1,2},{2,3},{3,4},{4,5},{5,6},{6,7},{7,8},{8,9},{9,10},{10,1... | collective-permute-start | bytes 1179656 | tf_op jit(solution)/shard_map/ppermute | solution.py:258
  6.4 0.8 %select_reduce_fusion.1 = s32[32]{0:T(128)S(1)} fusion(s32[32]{0:T(128)} %param.9), kind=kLoop, calls=%fused_computation.4 | loop fusion | flops 3040 | bytes 256 | tf_op jit(solution)/shard_map/reduce_sum | solution.py:21
  7.2 0.1 select_reduce_fusion
  7.3 0.1 copy.12
  7.5 0.0 collective-permute-done.1
  7.5 0.1 copy.13
  7.6 0.1 slice_multiply_fusion
  7.7 0.0 copy-start
  7.7 0.1 broadcast_in_dim.79
  7.8 0.1 broadcast_in_dim.77
  7.8 0.7 %gather_fusion = f32[256,16]{1,0:T(8,128)S(1)} fusion(f32[128,16]{1,0:T(8,128)S(1)} %get-tuple-element.6, s32[1024]{0:T(1024)S(1)} %pad_clamp_fusion), kind=kCustom, calls=%fused_computation | custom fusion | bytes 33792 | tf_op jit(solution)/shard_map/jit(_take)/gather | solution.py:273
  8.6 0.1 copy.14
  8.7 7.9 %collective-permute-done.halo_ref = bf16[3,8,8192]{2,1,0:T(8,128)(2,1)S(1)} collective-permute-done((bf16[3,8,8192]{2,1,0:T(8,128)(2,1)S(1)}, bf16[3,8,8192]{2,1,0:T(8,128)(2,1)S(1)}, u32[]{:S(2)}, u32[]{:S(2)}) %collective-permute-start) | collective-permute-done | bytes 393248 | tf_op jit(solution)/shard_map/ppermute | solution.py:258
  16.5 0.2 broadcast_in_dim.73.mask_ref
  16.7 0.3 broadcast_in_dim.78.decay_ref
  17.0 0.3 broadcast_in_dim.80.coef_ref
  17.4 0.0 copy-done
  17.4 30.6 %shard_map.55 = bf16[128,8192]{1,0:T(8,128)(2,1)S(1)} custom-call(bf16[3,128,8192]{2,1,0:T(8,128)(2,1)} %bitcast.8, bf16[3,8,8192]{2,1,0:T(8,128)(2,1)S(1)} %collective-permute-done.halo_ref, f32[3,7,8192]{2,1,0:T(8,128)S(1)} %copy-done, f32[7,128,128]{2,1,0:T(8,128)S(1)} %broadcast_in_dim.73.mask_ref, f32[2048,128]{1,0:T(8,128)S(1)} %broadcast_in_dim.78.decay_ref, ...), custom_call_target="tpu_custom_call" | custom-call | tf_op jit(solution)/shard_map/pallas_call | solution.py:275
  48.0 1.3 %copy.19 = bf16[128,8192]{1,0:T(8,128)(2,1)} copy(bf16[128,8192]{1,0:T(8,128)(2,1)S(1)} %shard_map.55) | data formatting | bytes 4194304
  (10 shorter events, 0.1 us)
Async XLA Ops:
  1.4 6.1 %collective-permute-start.1 = (f32[64,32]{0,1:T(8,128)S(1)}, f32[64,32]{0,1:T(8,128)S(1)}, u32[]{:S(2)}, u32[]{:S(2)}) collective-permute-start(f32[64,32]{0,1:T(8,128)S(1)} %constant_dynamic-update-slice_fusion), channel_id=1, source_target_pairs={{0,1},{1,0},{2,3},{3,2},{4,5},{5,4},{6,7},{7,6},{8,9},{9,8},{10,11... | collective-permute-start | bytes 24584 | tf_op jit(solution)/shard_map/ppermute | solution.py:244
  4.5 12.1 %collective-permute-start = (bf16[3,8,8192]{2,1,0:T(8,128)(2,1)S(1)}, bf16[3,8,8192]{2,1,0:T(8,128)(2,1)S(1)}, u32[]{:S(2)}, u32[]{:S(2)}) collective-permute-start(bf16[3,8,8192]{2,1,0:T(8,128)(2,1)S(1)} %slice.14), channel_id=1, source_target_pairs={{0,1},{1,2},{2,3},{3,4},{4,5},{5,6},{6,7},{7,8},{8,9},{9,10},{10,1... | collective-permute-start | bytes 1179656 | tf_op jit(solution)/shard_map/ppermute | solution.py:258
  7.7 9.7 %copy-start = (f32[3,7,8192]{2,1,0:T(8,128)S(1)}, f32[3,7,8192]{2,1,0:T(8,128)}, u32[]{:S(2)}) copy-start(f32[3,7,8192]{2,1,0:T(8,128)} %w_ref.1) | copy-start | bytes 2064388

commit v6 on v4

--- a/solution.py
+++ b/solution.py
@@ -234,13 +234,17 @@
 def everywhere(block, axis):
     n = lax.axis_size(axis)
     me = lax.axis_index(axis)
-    gathered = jnp.zeros((n,) + block.shape, block.dtype)
-    gathered = lax.dynamic_update_index_in_dim(gathered, block, me, 0)
+    held = [block]
     for shift in range(1, n):
-        arrived = lax.ppermute(block, axis, [(i, (i + shift) % n) for i in range(n)])
-        source = lax.rem(me - shift + n, n)
-        gathered = lax.dynamic_update_index_in_dim(gathered, arrived, source, 0)
-    return gathered.reshape((-1,) + block.shape[1:])
+        held.append(lax.ppermute(block, axis, [(i, (i + shift) % n) for i in range(n)]))
+
+    def of(owner):
+        shift = lax.rem(me - owner + n, n)
+        return lax.select_n(shift == 0, functools.reduce(
+            lambda found, s: jnp.where(shift == s, held[s], found), range(1, n), block
+        ), block)
+
+    return jnp.concatenate([of(owner) for owner in range(n)], axis=0)
 
 
 def shards(proj, conv_weight, residues, decays, doc_lengths):

time: 50.1 us -> 50.1 us (level)
    unnamed x4 -> x5, local copies, waits for them, and re-layouts: 2.03 us -> 2.12 us
  transfers between devices with their start and end apart: 2 -> 2, of which waited for: 1 -> 1; matrix products, arithmetic and copies ran while one was open for 6% -> 7% of each run, Pallas kernels for 0% -> 0%
where the time goes in v6:
time: 50.1 us; the launch traced here: 49.3 us
  Pallas kernels  30.6 us (61%)
  waiting for transfers between devices  7.85 us (16%)
  local copies, waits for them, and re-layouts  5.72 us (11%)
  starting transfers between devices  3.96 us (8%)
  other arithmetic  1.03 us (2%)
    pallas_call x1, Pallas kernels, shards(): pl.pallas_call(functools.partial(mixer_kernel, (modes, devices, mp, share...  30.6 us
    ppermute x1, waiting for transfers between devices, shards(): lax.ppermute(x[:, rows - HALO:], AXES, [(i, i + 1) for i in range(devices...  7.85 us
    unnamed x5, local copies, waits for them, and re-layouts  2.12 us
    ppermute x1, starting transfers between devices, everywhere(): lax.ppermute(block, axis, [(i, (i + shift) % n) for i in range(n)])  2.04 us
    ppermute x1, starting transfers between devices, shards(): lax.ppermute(x[:, rows - HALO:], AXES, [(i, i + 1) for i in range(devices...  1.92 us
    slice x1, local copies, waits for them, and re-layouts, shards(): x[:, rows - HALO:]  1.02 us
  transfers between devices with their start and end apart: 2, of which 1 were waited for; matrix products, arithmetic and copies ran while one was open for 7% of the time, Pallas kernels for 0%

profile of v6, /device:TPU:1, one launch (start us, length us, event | category | flops | bytes accessed | tf_op | source)
XLA Modules:
  0.0 49.3 jit_solution(18291919466905099837)
XLA Ops:
  0.0 0.7 %constant_dynamic-update-slice_fusion.1 = f32[64,32]{0,1:T(8,128)S(1)} fusion(f32[64,16]{0,1:T(8,128)} %param.7), kind=kLoop, calls=%fused_computation.15 | loop fusion | bytes 12288
  0.7 0.7 %constant_dynamic-update-slice_fusion = f32[64,32]{0,1:T(8,128)S(1)} fusion(f32[64,32]{0,1:T(8,128)S(1)} %constant_dynamic-update-slice_fusion.1, f32[64,16]{0,1:T(8,128)} %param.8), kind=kLoop, calls=%fused_computation.14 | loop fusion | bytes 12288 | tf_op jit(solution)/shard_map/concatenate | solution.py:259
  1.4 2.0 %collective-permute-start.1 = (f32[64,32]{0,1:T(8,128)S(1)}, f32[64,32]{0,1:T(8,128)S(1)}, u32[]{:S(2)}, u32[]{:S(2)}) collective-permute-start(f32[64,32]{0,1:T(8,128)S(1)} %constant_dynamic-update-slice_fusion), channel_id=1, source_target_pairs={{0,1},{1,0},{2,3},{3,2},{4,5},{5,4},{6,7},{7,6},{8,9},{9,8},{10,11... | collective-permute-start | bytes 24584 | tf_op jit(solution)/shard_map/ppermute | solution.py:239
  3.4 1.0 %slice.14 = bf16[3,8,8192]{2,1,0:T(8,128)(2,1)S(1)} slice(bf16[3,128,8192]{2,1,0:T(8,128)(2,1)} %bitcast.4), slice={[0:3], [120:128], [0:8192]} | slice | bytes 786432 | tf_op jit(solution)/shard_map/slice | solution.py:258
  4.5 1.9 %collective-permute-start = (bf16[3,8,8192]{2,1,0:T(8,128)(2,1)S(1)}, bf16[3,8,8192]{2,1,0:T(8,128)(2,1)S(1)}, u32[]{:S(2)}, u32[]{:S(2)}) collective-permute-start(bf16[3,8,8192]{2,1,0:T(8,128)(2,1)S(1)} %slice.14), channel_id=1, source_target_pairs={{0,1},{1,2},{2,3},{3,4},{4,5},{5,6},{6,7},{7,8},{8,9},{9,10},{10,1... | collective-permute-start | bytes 1179656 | tf_op jit(solution)/shard_map/ppermute | solution.py:258
  6.4 0.8 %select_reduce_fusion.1 = s32[32]{0:T(128)S(1)} fusion(s32[32]{0:T(128)} %param.9), kind=kLoop, calls=%fused_computation.8 | loop fusion | flops 3040 | bytes 256 | tf_op jit(solution)/shard_map/reduce_sum | solution.py:21
  7.2 0.1 select_reduce_fusion
  7.4 0.0 collective-permute-done.1
  7.4 0.1 pad_maximum_fusion
  7.5 0.1 copy.16
  7.6 0.1 copy.18
  7.7 0.1 broadcast_in_dim.64
  7.7 0.0 copy-start
  7.8 0.1 broadcast_in_dim.66
  7.9 0.7 %gather_fusion = f32[256,16]{1,0:T(8,128)S(1)} fusion(f32[128,16]{1,0:T(8,128)S(1)} %copy.18, s32[1024]{0:T(1024)S(1)} %pad_clamp_fusion), kind=kCustom, calls=%fused_computation | custom fusion | bytes 33792 | tf_op jit(solution)/shard_map/jit(_take)/gather | solution.py:273
  8.6 0.1 copy.17
  8.7 7.8 %collective-permute-done.halo_ref = bf16[3,8,8192]{2,1,0:T(8,128)(2,1)S(1)} collective-permute-done((bf16[3,8,8192]{2,1,0:T(8,128)(2,1)S(1)}, bf16[3,8,8192]{2,1,0:T(8,128)(2,1)S(1)}, u32[]{:S(2)}, u32[]{:S(2)}) %collective-permute-start) | collective-permute-done | bytes 393248 | tf_op jit(solution)/shard_map/ppermute | solution.py:258
  16.5 0.2 broadcast_in_dim.63.mask_ref
  16.7 0.3 broadcast_in_dim.65.decay_ref
  17.0 0.3 broadcast_in_dim.67.coef_ref
  17.4 0.0 copy-done
  17.4 30.6 %shard_map.55 = bf16[128,8192]{1,0:T(8,128)(2,1)S(1)} custom-call(bf16[3,128,8192]{2,1,0:T(8,128)(2,1)} %bitcast.5, bf16[3,8,8192]{2,1,0:T(8,128)(2,1)S(1)} %collective-permute-done.halo_ref, f32[3,7,8192]{2,1,0:T(8,128)S(1)} %copy-done, f32[7,128,128]{2,1,0:T(8,128)S(1)} %broadcast_in_dim.63.mask_ref, f32[2048,128]{1,0:T(8,128)S(1)} %broadcast_in_dim.65.decay_ref, ...), custom_call_target="tpu_custom_call" | custom-call | tf_op jit(solution)/shard_map/pallas_call | solution.py:275
  48.0 1.3 %copy.21 = bf16[128,8192]{1,0:T(8,128)(2,1)} copy(bf16[128,8192]{1,0:T(8,128)(2,1)S(1)} %shard_map.55) | data formatting | bytes 4194304
  (9 shorter events, 0.1 us)
Async XLA Ops:
  1.4 6.0 %collective-permute-start.1 = (f32[64,32]{0,1:T(8,128)S(1)}, f32[64,32]{0,1:T(8,128)S(1)}, u32[]{:S(2)}, u32[]{:S(2)}) collective-permute-start(f32[64,32]{0,1:T(8,128)S(1)} %constant_dynamic-update-slice_fusion), channel_id=1, source_target_pairs={{0,1},{1,0},{2,3},{3,2},{4,5},{5,4},{6,7},{7,6},{8,9},{9,8},{10,11... | collective-permute-start | bytes 24584 | tf_op jit(solution)/shard_map/ppermute | solution.py:239
  4.5 12.1 %collective-permute-start = (bf16[3,8,8192]{2,1,0:T(8,128)(2,1)S(1)}, bf16[3,8,8192]{2,1,0:T(8,128)(2,1)S(1)}, u32[]{:S(2)}, u32[]{:S(2)}) collective-permute-start(bf16[3,8,8192]{2,1,0:T(8,128)(2,1)S(1)} %slice.14), channel_id=1, source_target_pairs={{0,1},{1,2},{2,3},{3,4},{4,5},{5,6},{6,7},{7,8},{8,9},{9,10},{10,1... | collective-permute-start | bytes 1179656 | tf_op jit(solution)/shard_map/ppermute | solution.py:258
  7.7 9.6 %copy-start = (f32[3,7,8192]{2,1,0:T(8,128)S(1)}, f32[3,7,8192]{2,1,0:T(8,128)}, u32[]{:S(2)}) copy-start(f32[3,7,8192]{2,1,0:T(8,128)} %w_ref.1) | copy-start | bytes 2064388
